TPU v7x, 256 devices: a whole 4x4x8 slice. The times are simulated.
256 devices in a mesh: atoms: 32 (over x, z), samples: 8 (over y, core).
Axes of the slice: x: 4, y: 4, z: 8, core: 2. Of those that a mesh axis runs over, the one named last changes fastest.
Arguments:
- token_feats: bfloat16 [8192, 768], P('atoms', 'samples'), may hold values from -6 to 6
- proj_w: bfloat16 [768, 128], P('samples'), may hold values from -0.21875 to 0.21875
- atom_single: bfloat16 [65536, 128], P('atoms'), may hold values from -6 to 6
- atom_token: int32 [65536], P('atoms'), may hold values from 0 to 8191, as said below
- true_coords: float32 [3, 65536], P(None, 'atoms'), may hold values from -12 to 12
- noise: float32 [8, 3, 65536], P('samples', None, 'atoms'), may hold values from -6 to 6
- sigma: float32 [8], P('samples'), may hold values from 0.5 to 4
- coord_in: float32 [3, 128], replicated, may hold values from -3.5 to 3.5
- w_qkv: bfloat16 [3, 128, 384], replicated, as said below
- w_o: bfloat16 [3, 128, 128], replicated, may hold values from -0.5 to 0.5
- w_gu: bfloat16 [3, 128, 512], replicated, may hold values from -0.5 to 0.5
- w_down: bfloat16 [3, 256, 128], replicated, may hold values from -0.375 to 0.375
- gains: float32 [3, 2, 128], replicated, may hold values from 0.1 to 1.9
- w_out: float32 [128, 3], replicated, may hold values from -0.5 to 0.5
- pair_blocks: int32 [512, 13], P('atoms'), may hold values from 0 to 511, as said below
- pair_count: int32 [512], P('atoms'), may hold values from 1 to 13, as said below
Outputs:
- coord_grad: float32 [8, 3, 65536], P('samples', None, 'atoms')
- lddt_grad: float32 [8, 3, 65536], P('samples', None, 'atoms')
Inputs may be any that keep to these rules, and one draw needn't show every extreme that they name: `atom_token`: atom a belongs to a token that differs from a // 8 by at most 16 before clipping to the token range; in each aligned run of 2048 atoms the first atom is -16 and the last +16 from that value before clipping. `pair_blocks`: the first pair_count[b] entries of row b are distinct blocks, the first being b itself; entries past pair_count[b] are b. Listing is symmetric: c is among the live entries of row b exactly when b is among the live entries of row c. `pair_count`: some block has 13 live entries. `w_qkv`: Queries, keys and values stand side by side along the last dimension.
All inputs are finite; a program needn't handle non-finite values.
Results may differ from a plain program's by a relative error of at most 0.018.
Values may be sent and summed in bfloat16 or wider, within the bound.
A program may use at most 64 MiB of HBM per device.

v0:
```python
import functools
import math

import jax
import jax.numpy as jnp
from jax import lax
from jax.experimental import pallas as pl
from jax.experimental.pallas import tpu as pltpu
from jax.sharding import PartitionSpec as P

HEADS = 4
HEAD_DIM = 32
FF_ATOM = 256
LAYERS = 3
QBLK = 32
KWIN = 128
PAIR_BLK = 128
CHANNELS = 128
CHUNK = 256
HALO = 256
TOK_HALO = 48
TOK_WIN = 64
EPS = 1e-05
VMEM_LIMIT = 56 * 1024 * 1024

f32 = jnp.float32
bf16 = jnp.bfloat16


def dot(a, b, dims=((1,), (0,)), precision=None):
    return lax.dot_general(a, b, (dims, ((), ())), precision=precision, preferred_element_type=f32)


def pieces(v):
    hi = v.astype(bf16).astype(f32)
    mid = (v - hi).astype(bf16).astype(f32)
    lo = (v - hi - mid).astype(bf16).astype(f32)
    return hi, mid, lo


def rms_scale(h):
    return h * lax.rsqrt(jnp.mean(h * h, axis=1, keepdims=True) + EPS)


def atoms_kernel(
    place, scal, single, cx, tok, coord_w, wqkv, wo, wgu, wdown, gains, wout,
    pred, hid, qkv, bias,
):
    rows = single.shape[0] - 2 * HALO
    ext = single.shape[0]
    first_atom = place[0]
    total_atoms = place[1]
    first_tok = place[2]
    q_scale = math.log2(math.e) / math.sqrt(HEAD_DIM)
    lane = lax.broadcasted_iota(jnp.int32, (1, CHANNELS), 1) // HEAD_DIM

    pos = first_atom - HALO + lax.broadcasted_iota(jnp.int32, (ext, CHANNELS), 0)
    bias[...] = jnp.where((pos >= 0) & (pos < total_atoms), 0.0, -1e30)

    def project(layer, at, h):
        normed = (rms_scale(h) * gains[2 * layer : 2 * layer + 1, :]).astype(bf16)
        out = dot(normed, wqkv[layer])
        rows_at = pl.ds(at, h.shape[0])
        qkv[layer % 2, rows_at, 0:128] = (out[:, :128] * q_scale).astype(bf16)
        qkv[layer % 2, rows_at, 128:384] = out[:, 128:].astype(bf16)

    def first(k, _):
        at = pl.multiple_of(k * CHUNK, CHUNK)
        c = cx[:, pl.ds(at, CHUNK)]
        hi, mid, lo = pieces(c)
        rel = c[3:4, :].astype(jnp.int32) - (first_tok - TOK_HALO + k * (CHUNK // 8))
        hot = jnp.where(lax.broadcasted_iota(jnp.int32, (TOK_WIN, CHUNK), 0) == rel, 1.0, 0.0)
        left = jnp.concatenate([hot, hi, hi, hi, mid, mid, lo], axis=0).astype(bf16)
        tok_at = pl.ds(pl.multiple_of(k * (CHUNK // 8), CHUNK // 8), TOK_WIN)
        right = jnp.concatenate([tok[tok_at, :], coord_w[...]], axis=0)
        h = single[pl.ds(at, CHUNK), :].astype(f32) + dot(left, right, ((0,), (0,)))
        hid[pl.ds(at, CHUNK), :] = h
        project(0, at, h)
        return 0

    lax.fori_loop(0, ext // CHUNK, first, 0)

    def attend(layer, at, size):
        buf = layer % 2
        outs = []
        for w in range(size // QBLK):
            q = qkv[buf, pl.ds(at + w * QBLK, QBLK), 0:128]
            keys_at = pl.ds(at + (w * QBLK - 48), KWIN)
            keys = qkv[buf, keys_at, 128:256]
            values = qkv[buf, keys_at, 256:384]
            zero = jnp.zeros_like(q)
            spread = jnp.concatenate([jnp.where(lane == h, q, zero) for h in range(HEADS)], axis=0)
            scores = dot(keys, spread, ((1,), (1,))) + bias[keys_at, :]
            top = jnp.max(scores, axis=0, keepdims=True)
            weights = jnp.exp2(scores - top)
            weights = (weights * (1.0 / jnp.sum(weights, axis=0, keepdims=True))).astype(bf16)
            both = dot(weights, values, ((0,), (0,)))
            out = both[0:QBLK]
            for h in range(1, HEADS):
                out = jnp.where(lane == h, both[h * QBLK : (h + 1) * QBLK], out)
            outs.append(out.astype(bf16))
        return jnp.concatenate(outs, axis=0)

    def block(layer, at, size):
        h = hid[pl.ds(at, size), :]
        h = h + dot(attend(layer, at, size), wo[layer])
        normed = (rms_scale(h) * gains[2 * layer + 1 : 2 * layer + 2, :]).astype(bf16)
        gu = dot(normed, wgu[layer])
        half = 0.5 * gu[:, :FF_ATOM]
        inner = (half * (1.0 + jnp.tanh(half)) * gu[:, FF_ATOM:]).astype(bf16)
        h = h + dot(inner, wdown[layer])
        if layer + 1 < LAYERS:
            hid[pl.ds(at, size), :] = h
            project(layer + 1, at, h)
        else:
            update = dot(wout[...], rms_scale(h), ((1,), (1,)), lax.Precision.HIGHEST)
            noisy = cx[:, pl.ds(at, size)]
            pred[:, pl.ds(pl.multiple_of(at - HALO, size), size)] = scal[0] * noisy + scal[1] * update

    for layer in range(LAYERS):
        low = HALO if layer == LAYERS - 1 else HALO - 128
        span = rows if layer == LAYERS - 1 else rows + 256

        def step(k, _, layer=layer, low=low):
            block(layer, pl.multiple_of(low + k * CHUNK, 128), CHUNK)
            return 0

        lax.fori_loop(0, span // CHUNK, step, 0)


def pairs_kernel(
    scal, counts, partners, gathered_pred, gathered_true, pred, true,
    coord_grad, lddt_grad, wide_pred, wide_true,
):
    blocks = counts.shape[0]
    me = partners[0, 0] // blocks * blocks
    wide_pred[...] = gathered_pred[...].astype(f32)
    wide_true[...] = gathered_true[...].astype(f32)
    row8 = lax.broadcasted_iota(jnp.int32, (8, PAIR_BLK), 0)
    row4 = row8 & 3
    diff = lax.broadcasted_iota(jnp.int32, (PAIR_BLK, PAIR_BLK), 0) - lax.broadcasted_iota(
        jnp.int32, (PAIR_BLK, PAIR_BLK), 1
    )

    def partner_rows(wide, p):
        base = p // blocks * (3 * blocks) + p % blocks
        x, y, z = (wide[pl.ds(base + d * blocks, 1), :] for d in range(3))
        n1, n2, n3 = pieces(x * x + y * y + z * z)
        xyz = jnp.where(row4 == 0, x, jnp.where(row4 == 1, y, z))
        upper = jnp.where(row4 == 3, jnp.where(row8 == 3, n1, n2), xyz)
        ones = jnp.where(row8 < 7, 1.0, 0.0)
        lower = jnp.where(row8 < 3, xyz, jnp.where(row8 == 3, n3, ones))
        return jnp.concatenate([upper, lower], axis=0)

    def own_rows(x, y, z):
        n = x * x + y * y + z * z + 1.0
        n1, n2, n3 = pieces(0.25 * n)
        xp, yp, zp = pieces(-0.5 * x), pieces(-0.5 * y), pieces(-0.5 * z)

        def xyz(i):
            return jnp.where(row4 == 0, xp[i], jnp.where(row4 == 1, yp[i], zp[i]))

        upper = jnp.where(row4 == 3, 0.25, jnp.where(row8 < 4, xyz(0), xyz(1)))
        norms = jnp.where(row8 == 4, n1, jnp.where(row8 == 5, n2, n3))
        norms = jnp.where(row8 == 7, 0.0, norms)
        lower = jnp.where(row8 < 3, xyz(2), jnp.where(row8 == 3, 0.25, norms))
        return jnp.concatenate([upper, lower], axis=0)

    def visit(b, _):
        at = pl.ds(pl.multiple_of(b * PAIR_BLK, PAIR_BLK), PAIR_BLK)
        px, py, pz = (pred[d : d + 1, at] for d in range(3))
        tx, ty, tz = (true[d : d + 1, at] for d in range(3))
        none = jnp.zeros((16, PAIR_BLK), f32)
        own = jnp.concatenate(
            [
                jnp.concatenate([own_rows(px, py, pz), none], axis=1),
                jnp.concatenate([none, own_rows(tx, ty, tz)], axis=1),
            ],
            axis=0,
        ).astype(bf16)

        def tile(m, total):
            p = partners[b, m]
            part_pred = partner_rows(wide_pred, p)
            part = jnp.concatenate([part_pred, partner_rows(wide_true, p)], axis=0).astype(bf16)
            squares = dot(part, own, ((0,), (0,)))
            sp, st = squares[:, :PAIR_BLK], squares[:, PAIR_BLK:]
            rp = lax.rsqrt(sp)
            gap = sp * rp - st * lax.rsqrt(st)
            e2 = gap * gap + 0.0025
            re = lax.rsqrt(e2)
            err = e2 * re
            th = [jnp.tanh(0.5 * t - err) for t in (0.5, 1.0, 2.0, 4.0)]
            slope = 4.0 - (th[0] * th[0] + th[1] * th[1] + th[2] * th[2] + th[3] * th[3])
            coef = slope * gap * (re * rp)
            shut = jnp.where(m == 0, 0, 2 * PAIR_BLK)
            coef = jnp.where(diff == shut, 0.0, coef)
            sums = dot(part[0:16], coef.astype(bf16))
            return total + sums[8:16]

        total = lax.fori_loop(0, counts[b], tile, jnp.zeros((8, PAIR_BLK), f32))
        for d, (pc, tc) in enumerate(((px, tx), (py, ty), (pz, tz))):
            lg = scal[0] * (pc * total[4:5] - total[d : d + 1])
            lddt_grad[0, d : d + 1, at] = lg
            coord_grad[0, d : d + 1, at] = scal[1] * (pc - tc) - lg * (1.0 / PAIR_BLK)
        return 0

    lax.fori_loop(0, blocks, visit, 0)


def vmem(n):
    return [pl.BlockSpec(memory_space=pltpu.VMEM)] * n


def smem(n):
    return [pl.BlockSpec(memory_space=pltpu.SMEM)] * n


def run_atoms(place, scal, single, cx, tok, coord_in, w_qkv, w_o, w_gu, w_down, gains, w_out):
    ext = single.shape[0]
    rows = ext - 2 * HALO
    c3 = jnp.pad(coord_in, ((0, 5), (0, 0)))
    hi, mid, lo = (lax.reduce_precision(c3, 8, 7), None, None)
    rest = c3 - hi
    mid = lax.reduce_precision(rest, 8, 7)
    lo = rest - mid
    coord_w = jnp.concatenate([hi, mid, lo, hi, mid, hi], axis=0).astype(bf16)
    gains8 = jnp.pad(gains.reshape(2 * LAYERS, CHANNELS), ((0, 2), (0, 0)))
    wout8 = jnp.pad(w_out.T, ((0, 5), (0, 0)))
    return pl.pallas_call(
        atoms_kernel,
        name="atoms",
        out_shape=jax.ShapeDtypeStruct((8, rows), f32),
        in_specs=smem(2) + vmem(10),
        out_specs=pl.BlockSpec(memory_space=pltpu.VMEM),
        scratch_shapes=[
            pltpu.VMEM((ext, CHANNELS), f32),
            pltpu.VMEM((2, ext, 3 * CHANNELS), bf16),
            pltpu.VMEM((ext, CHANNELS), f32),
        ],
        compiler_params=pltpu.CompilerParams(vmem_limit_bytes=VMEM_LIMIT),
    )(place, scal, single, cx, tok, coord_w, w_qkv, w_o, w_gu, w_down, gains8, wout8)


def run_pairs(scal, counts, partners, gathered_pred, gathered_true, pred, true):
    rows = pred.shape[1]
    wide = pltpu.VMEM(gathered_pred.shape, f32)
    out = jax.ShapeDtypeStruct((1, 3, rows), f32)
    return pl.pallas_call(
        pairs_kernel,
        name="pairs",
        out_shape=(out, out),
        in_specs=smem(3) + vmem(4),
        out_specs=tuple(vmem(2)),
        scratch_shapes=[wide, wide],
        compiler_params=pltpu.CompilerParams(vmem_limit_bytes=VMEM_LIMIT),
    )(scal, counts, partners, gathered_pred, gathered_true, pred, true)


def extended(value, axis, dim, width):
    peers, length = (lax.axis_size(axis), value.shape[dim])
    up = [(i, (i + 1) % peers) for i in range(peers)]
    down = [(j, i) for i, j in up]
    last = lax.slice_in_dim(value, length - width, length, axis=dim)
    first = lax.slice_in_dim(value, 0, width, axis=dim)
    before = lax.ppermute(last, axis, up)
    after = lax.ppermute(first, axis, down)
    return jnp.concatenate([before, value, after], axis=dim)


def on_device(
    token_feats, proj_w, atom_single, atom_token, true_coords, noise, sigma, coord_in,
    w_qkv, w_o, w_gu, w_down, gains, w_out, pair_blocks, pair_count,
):
    rank = lax.axis_index("atoms")
    tok_rows = token_feats.shape[0]
    rows = atom_single.shape[0]
    total_atoms = rows * lax.axis_size("atoms")
    whole_feats = lax.all_gather(token_feats, "samples", axis=1, tiled=True)
    whole_proj = lax.all_gather(proj_w, "samples", axis=0, tiled=True)
    token_proj = jnp.dot(whole_feats, whole_proj, preferred_element_type=f32).astype(bf16)
    tok = extended(token_proj, "atoms", 0, TOK_HALO)
    single = extended(atom_single, "atoms", 0, HALO)
    sig = sigma[0]
    noise_total = sig * sig + 4.0
    root = jnp.sqrt(noise_total)
    scaled = (true_coords + sig * noise[0]) / root
    cx = jnp.concatenate(
        [scaled, atom_token.astype(f32)[None], jnp.zeros((4, rows), f32)], axis=0
    )
    cx = extended(cx, "atoms", 1, HALO)
    place = jnp.stack([rank * rows, jnp.int32(total_atoms), rank * tok_rows]).astype(jnp.int32)
    scal = jnp.stack([4.0 / root, 2.0 * sig / root])
    pred = run_atoms(place, scal, single, cx, tok, coord_in, w_qkv, w_o, w_gu, w_down, gains, w_out)

    def everyone(v):
        return lax.all_gather(v[:3].astype(bf16).reshape(-1, PAIR_BLK), "atoms", axis=0, tiled=True)

    total_count = lax.psum(jnp.sum(pair_count), "atoms").astype(f32)
    pair_total = total_count * (PAIR_BLK * PAIR_BLK) - PAIR_BLK * (total_atoms // PAIR_BLK)
    scal2 = jnp.stack(
        [total_atoms * PAIR_BLK / pair_total * (-0.0625), 2.0 / 3.0 * noise_total / (2.0 * sig) ** 2]
    )
    return run_pairs(
        scal2, pair_count, pair_blocks, everyone(pred), everyone(true_coords), pred, true_coords
    )


def solution(mesh):
    in_specs = (
        P("atoms", "samples"),
        P("samples", None),
        P("atoms", None),
        P("atoms"),
        P(None, "atoms"),
        P("samples", None, "atoms"),
        P("samples"),
        P(), P(), P(), P(), P(), P(), P(),
        P("atoms", None),
        P("atoms"),
    )
    out_specs = (P("samples", None, "atoms"), P("samples", None, "atoms"))
    return jax.shard_map(on_device, mesh=mesh, in_specs=in_specs, out_specs=out_specs, check_vma=False)
```

profile of v0, /device:TPU:230, one launch (start us, length us, event | category | flops | bytes accessed | tf_op | source)
XLA Modules:
  0.0 329.4 jit_solution(16459681904581164746)
XLA Ops:
  0.6 0.0 copy-start.2
  1.3 0.7 convert_element_type.20
  2.0 0.9 fusion.4
  2.9 0.1 collective-permute-start.2
  3.0 0.0 copy-start
  3.0 2.0 collective-permute-start.3
  5.0 13.7 %all_gather.12 = bf16[256,768]{0,1:T(8,128)(2,1)S(1)} all-gather(bf16[256,96]{0,1:T(8,128)(2,1)} %param.16), channel_id=1, replica_groups=mesh['atoms'=32,'samples'=8] {'samples'}, dimensions={1}, use_global_device_ids=true | all-gather | bytes 442368 | tf_op jit(solution)/shard_map/all_gather | solution.py:279
  18.7 0.0 copy-done.2
  18.7 0.0 copy-start.1
  18.7 0.0 copy-start.6
  18.7 12.9 %all_gather.13 = bf16[768,128]{1,0:T(8,128)(2,1)S(1)} all-gather(bf16[96,128]{1,0:T(8,128)(2,1)S(1)} %copy-done.2), channel_id=1, replica_groups=mesh['atoms'=32,'samples'=8] {'samples'}, dimensions={0}, use_global_device_ids=true | all-gather | bytes 221184 | tf_op jit(solution)/shard_map/all_gather | solution.py:280
  31.7 0.0 copy-start.4
  31.7 0.0 copy-start.5
  31.7 0.3 convolution_convert_fusion
  32.0 3.5 %collective-permute-start.4 = (bf16[48,128]{1,0:T(8,128)(2,1)S(1)}, bf16[48,128]{1,0:T(8,128)(2,1)S(1)}, u32[]{:S(2)}, u32[]{:S(2)}) collective-permute-start(bf16[48,128]{1,0:T(8,128)(2,1)S(1)} %get-tuple-element.8), channel_id=1, source_target_pairs={{0,8},{8,16},{16,24},{24,32},{32,40},{40,48},{48,56},{56,64},{64,7... | collective-permute-start | bytes 36872 | tf_op jit(solution)/shard_map/ppermute | solution.py:266
  35.5 0.0 collective-permute-start.5
  35.5 0.0 copy-done
  35.5 5.4 %collective-permute-start = (bf16[256,128]{1,0:T(8,128)(2,1)S(1)}, bf16[256,128]{1,0:T(8,128)(2,1)S(1)}, u32[]{:S(2)}, u32[]{:S(2)}) collective-permute-start(bf16[256,128]{1,0:T(8,128)(2,1)S(1)} %get-tuple-element.4), channel_id=1, source_target_pairs={{0,8},{8,16},{16,24},{24,32},{32,40},{40,48},{48,56},{56,64},{64,7... | collective-permute-start | bytes 196616 | tf_op jit(solution)/shard_map/ppermute | solution.py:266
  41.0 0.0 copy-done.1
  41.1 0.0 copy-done.6
  41.1 0.0 copy-start.3
  41.1 0.6 reduce_sum.9
  41.8 15.1 %psum.7 = s32[]{:T(128)} all-reduce(s32[]{:T(128)} %reduce_sum.9), channel_id=1, replica_groups=mesh['atoms'=32,'samples'=8] {'atoms'}, use_global_device_ids=true, to_apply=%region_1.2 | all-reduce | flops 1 | bytes 8 | tf_op jit(solution)/shard_map/psum | solution.py:299
  57.6 0.6 pad_maximum_fusion.7.scal
  58.3 0.6 pad_maximum_fusion.6.scal
  58.9 0.6 pad_add_fusion.place
  59.4 55.2 %all_gather.15.gathered_true = bf16[1536,128]{1,0:T(8,128)(2,1)} all-gather(bf16[48,128]{1,0:T(8,128)(2,1)S(1)} %reshape.17), channel_id=1, replica_groups=mesh['atoms'=32,'samples'=8] {'atoms'}, dimensions={0}, use_global_device_ids=true | all-gather | bytes 405504 | tf_op jit(solution)/shard_map/all_gather | solution.py:297
  114.7 0.0 copy-done.4
  114.7 0.6 pad.12.gains
  115.3 0.0 copy-done.5
  115.3 0.6 pad.13.wout
  115.9 0.0 collective-permute-done.2
  115.9 0.0 collective-permute-start.1
  115.9 0.0 collective-permute-done.3
  115.9 0.7 pad_maximum_fusion.2.cx
  116.6 0.0 collective-permute-done.4
  116.6 0.0 collective-permute-done.5
  116.6 0.6 pad_maximum_fusion.1.tok
  117.2 0.0 collective-permute-done
  117.2 6.3 %collective-permute-done.1 = bf16[256,128]{1,0:T(8,128)(2,1)S(1)} collective-permute-done((bf16[256,128]{1,0:T(8,128)(2,1)S(1)}, bf16[256,128]{1,0:T(8,128)(2,1)S(1)}, u32[]{:S(2)}, u32[]{:S(2)}) %collective-permute-start.1) | collective-permute-done | bytes 65568 | tf_op jit(solution)/shard_map/ppermute | solution.py:267
  123.5 0.9 pad_maximum_fusion.single
  124.4 0.0 copy-done.3
  124.4 85.7 %atoms.1.pred = f32[8,2048]{1,0:T(8,128)} custom-call(s32[3]{0:T(128)} %pad_add_fusion.place, f32[2]{0:T(128)} %pad_maximum_fusion.7.scal, bf16[2560,128]{1,0:T(8,128)(2,1)} %pad_maximum_fusion.single, f32[8,2560]{1,0:T(8,128)} %pad_maximum_fusion.2.cx, bf16[352,128]{1,0:T(8,128)(2,1)} %pad_maximum_fusion.1.tok, bf16[48,128]{1,0:T(8,128)(2,1)} %copy-done.3, ...), custom_call_target="tpu_custom_call" | custom-call | tf_op jit(solution)/shard_map/atoms/pallas_call | solution.py:230
  210.1 0.8 slice.33
  211.0 50.6 %all_gather.14.gathered_pred = bf16[1536,128]{1,0:T(8,128)(2,1)} all-gather(bf16[48,128]{1,0:T(8,128)(2,1)S(1)} %reshape.16), channel_id=1, replica_groups=mesh['atoms'=32,'samples'=8] {'atoms'}, dimensions={0}, use_global_device_ids=true | all-gather | bytes 405504 | tf_op jit(solution)/shard_map/all_gather | solution.py:297
  261.6 65.1 %pairs.1 = (f32[1,3,2048]{2,1,0:T(4,128)}, f32[1,3,2048]{2,1,0:T(4,128)}) custom-call(f32[2]{0:T(128)} %pad_maximum_fusion.6.scal, s32[16]{0:T(128)} %counts.1, s32[16,13]{1,0:T(8,128)} %partners.1, bf16[1536,128]{1,0:T(8,128)(2,1)} %all_gather.14.gathered_pred, bf16[1536,128]{1,0:T(8,128)(2,1)} %all_gather.15.gathered_true, f32[8,2048]{1,0:T(8,128)} %atoms.1.pred, ...), custom_call_target="tpu_custom_call" | custom-call | tf_op jit(solution)/shard_map/pairs/pallas_call | solution.py:249
  326.7 1.4 copy.19
  328.0 1.4 copy.20
  (13 shorter events, 0.2 us)
Async XLA Ops:
  0.6 18.1 %copy-start.2 = (bf16[96,128]{1,0:T(8,128)(2,1)S(1)}, bf16[96,128]{1,0:T(8,128)(2,1)}, u32[]{:S(2)}) copy-start(bf16[96,128]{1,0:T(8,128)(2,1)} %param.17) | copy-start | bytes 73732
  2.9 113.0 %collective-permute-start.2 = (f32[8,256]{1,0:T(8,128)S(1)}, f32[8,256]{1,0:T(8,128)S(1)}, u32[]{:S(2)}, u32[]{:S(2)}) collective-permute-start(f32[8,256]{1,0:T(8,128)S(1)} %get-tuple-element.6), channel_id=1, source_target_pairs={{0,8},{8,16},{16,24},{24,32},{32,40},{40,48},{48,56},{56,64},{64,7... | collective-permute-start | bytes 24584 | tf_op jit(solution)/shard_map/ppermute | solution.py:266
  3.0 32.5 %copy-start = (bf16[2048,128]{1,0:T(8,128)(2,1)S(1)}, bf16[2048,128]{1,0:T(8,128)(2,1)}, u32[]{:S(2)}) copy-start(bf16[2048,128]{1,0:T(8,128)(2,1)} %param.18) | copy-start | bytes 1572868
  3.0 112.9 %collective-permute-start.3 = (f32[8,256]{1,0:T(8,128)S(1)}, f32[8,256]{1,0:T(8,128)S(1)}, u32[]{:S(2)}, u32[]{:S(2)}) collective-permute-start(f32[8,256]{1,0:T(8,128)S(1)} %get-tuple-element.7), channel_id=1, source_target_pairs={{8,0},{16,8},{24,16},{32,24},{40,32},{48,40},{56,48},{64,56},{72,6... | collective-permute-start | bytes 24584 | tf_op jit(solution)/shard_map/ppermute | solution.py:267
  18.7 22.3 %copy-start.1 = (f32[3,128]{1,0:T(4,128)S(1)}, f32[3,128]{1,0:T(4,128)}, u32[]{:S(2)}) copy-start(f32[3,128]{1,0:T(4,128)} %param.23) | copy-start | bytes 4612
  18.7 22.4 %copy-start.6 = (s32[16]{0:T(128)S(1)}, s32[16]{0:T(128)}, u32[]{:S(2)}) copy-start(s32[16]{0:T(128)} %counts.1) | copy-start | bytes 196
  31.7 83.0 %copy-start.4 = (f32[3,2,128]{2,1,0:T(2,128)S(1)}, f32[3,2,128]{2,1,0:T(2,128)}, u32[]{:S(2)}) copy-start(f32[3,2,128]{2,1,0:T(2,128)} %param.28) | copy-start | bytes 9220
  31.7 83.7 %copy-start.5 = (f32[128,3]{0,1:T(4,128)S(1)}, f32[128,3]{0,1:T(4,128)}, u32[]{:S(2)}) copy-start(f32[128,3]{0,1:T(4,128)} %param.29) | copy-start | bytes 4612
  32.0 84.6 %collective-permute-start.4 = (bf16[48,128]{1,0:T(8,128)(2,1)S(1)}, bf16[48,128]{1,0:T(8,128)(2,1)S(1)}, u32[]{:S(2)}, u32[]{:S(2)}) collective-permute-start(bf16[48,128]{1,0:T(8,128)(2,1)S(1)} %get-tuple-element.8), channel_id=1, source_target_pairs={{0,8},{8,16},{16,24},{24,32},{32,40},{40,48},{48,56},{56,64},{64,7... | collective-permute-start | bytes 36872 | tf_op jit(solution)/shard_map/ppermute | solution.py:266
  35.5 81.1 %collective-permute-start.5 = (bf16[48,128]{1,0:T(8,128)(2,1)S(1)}, bf16[48,128]{1,0:T(8,128)(2,1)S(1)}, u32[]{:S(2)}, u32[]{:S(2)}) collective-permute-start(bf16[48,128]{1,0:T(8,128)(2,1)S(1)} %get-tuple-element.9), channel_id=1, source_target_pairs={{8,0},{16,8},{24,16},{32,24},{40,32},{48,40},{56,48},{64,56},{72,6... | collective-permute-start | bytes 36872 | tf_op jit(solution)/shard_map/ppermute | solution.py:267
  35.5 81.7 %collective-permute-start = (bf16[256,128]{1,0:T(8,128)(2,1)S(1)}, bf16[256,128]{1,0:T(8,128)(2,1)S(1)}, u32[]{:S(2)}, u32[]{:S(2)}) collective-permute-start(bf16[256,128]{1,0:T(8,128)(2,1)S(1)} %get-tuple-element.4), channel_id=1, source_target_pairs={{0,8},{8,16},{16,24},{24,32},{32,40},{40,48},{48,56},{56,64},{64,7... | collective-permute-start | bytes 196616 | tf_op jit(solution)/shard_map/ppermute | solution.py:266
  41.1 83.3 %copy-start.3 = (bf16[48,128]{1,0:T(8,128)(2,1)}, bf16[48,128]{1,0:T(8,128)(2,1)S(1)}, u32[]{:S(2)}) copy-start(bf16[48,128]{1,0:T(8,128)(2,1)S(1)} %constant_dynamic-update-slice_fusion.coord_w) | copy-start | bytes 36868
  115.9 7.6 %collective-permute-start.1 = (bf16[256,128]{1,0:T(8,128)(2,1)S(1)}, bf16[256,128]{1,0:T(8,128)(2,1)S(1)}, u32[]{:S(2)}, u32[]{:S(2)}) collective-permute-start(bf16[256,128]{1,0:T(8,128)(2,1)S(1)} %get-tuple-element.5), channel_id=1, source_target_pairs={{8,0},{16,8},{24,16},{32,24},{40,32},{48,40},{56,48},{64,56},{72,6... | collective-permute-start | bytes 196616 | tf_op jit(solution)/shard_map/ppermute | solution.py:267
where the time goes:
time: 330 us; the launch traced here: 329 us
  Pallas kernels  151 us (46%)
  blocking collectives  148 us (45%)
  starting transfers between devices  11 us (3%)
  waiting for transfers between devices  6.28 us (2%)
  other arithmetic  6.23 us (2%)
  local copies, waits for them, and re-layouts  4.94 us (1%)
    all_gather x2, blocking collectives, everyone(): lax.all_gather(v[:3].astype(bf16).reshape(-1, PAIR_BLK), 'atoms', axis=0,...  106 us
    pallas_call x1, Pallas kernels, run_atoms(): pl.pallas_call(atoms_kernel, name='atoms', out_shape=jax.ShapeDtypeStruct...  85.7 us
    pallas_call x1, Pallas kernels, run_pairs(): pl.pallas_call(pairs_kernel, name='pairs', out_shape=(out, out), in_specs...  65.1 us
    psum x1, blocking collectives, on_device(): total_count = lax.psum(jnp.sum(pair_count), 'atoms').astype(f32)  15.1 us
    all_gather x1, blocking collectives, on_device(): whole_feats = lax.all_gather(token_feats, 'samples', axis=1, tiled=True)  13.7 us
    all_gather x1, blocking collectives, on_device(): whole_proj = lax.all_gather(proj_w, 'samples', axis=0, tiled=True)  12.9 us
    ppermute x3, starting transfers between devices, extended(): before = lax.ppermute(last, axis, up)  9 us
  transfers between devices with their start and end apart: 6, of which 1 were waited for; matrix products, arithmetic and copies ran while one was open for 2% of the time, Pallas kernels for 0%

commit v1 on v0

--- a/solution.py
+++ b/solution.py
@@ -44,7 +44,7 @@
 
 def atoms_kernel(
     place, scal, single, cx, tok, coord_w, wqkv, wo, wgu, wdown, gains, wout,
-    pred, hid, qkv, bias,
+    pred, pay, hid, qkv, bias, wide,
 ):
     rows = single.shape[0] - 2 * HALO
     ext = single.shape[0]
@@ -115,7 +115,13 @@
         else:
             update = dot(wout[...], rms_scale(h), ((1,), (1,)), lax.Precision.HIGHEST)
             noisy = cx[:, pl.ds(at, size)]
-            pred[:, pl.ds(pl.multiple_of(at - HALO, size), size)] = scal[0] * noisy + scal[1] * update
+            out = scal[0] * noisy + scal[1] * update
+            pred[:, pl.ds(pl.multiple_of(at - HALO, size), size)] = out
+            first_block = (at - HALO) // PAIR_BLK
+            for i in range(size // PAIR_BLK):
+                for d in range(3):
+                    row = pl.ds(d * (rows // PAIR_BLK) + first_block + i, 1)
+                    wide[row, :] = out[d : d + 1, i * PAIR_BLK : (i + 1) * PAIR_BLK]
 
     for layer in range(LAYERS):
         low = HALO if layer == LAYERS - 1 else HALO - 128
@@ -126,6 +132,7 @@
             return 0
 
         lax.fori_loop(0, span // CHUNK, step, 0)
+    pay[...] = wide[...].astype(bf16)
 
 
 def pairs_kernel(
@@ -133,17 +140,23 @@
     coord_grad, lddt_grad, wide_pred, wide_true,
 ):
     blocks = counts.shape[0]
-    me = partners[0, 0] // blocks * blocks
     wide_pred[...] = gathered_pred[...].astype(f32)
     wide_true[...] = gathered_true[...].astype(f32)
+    peers = gathered_pred.shape[0] // (3 * blocks)
+    listed = jnp.zeros((blocks, PAIR_BLK), f32)
+    for peer in range(peers):
+        listed = listed + wide_true[peer * 4 * blocks + 3 * blocks : (peer + 1) * 4 * blocks, :]
+    listed = jnp.sum(listed, axis=0, keepdims=True)
+    total_pairs = listed * (PAIR_BLK * PAIR_BLK) - float(PAIR_BLK * blocks * peers)
+    pair_scale = -0.0625 * (blocks * peers * PAIR_BLK * PAIR_BLK) / total_pairs
     row8 = lax.broadcasted_iota(jnp.int32, (8, PAIR_BLK), 0)
     row4 = row8 & 3
     diff = lax.broadcasted_iota(jnp.int32, (PAIR_BLK, PAIR_BLK), 0) - lax.broadcasted_iota(
         jnp.int32, (PAIR_BLK, PAIR_BLK), 1
     )
 
-    def partner_rows(wide, p):
-        base = p // blocks * (3 * blocks) + p % blocks
+    def partner_rows(wide, p, per):
+        base = p // blocks * (per * blocks) + p % blocks
         x, y, z = (wide[pl.ds(base + d * blocks, 1), :] for d in range(3))
         n1, n2, n3 = pieces(x * x + y * y + z * z)
         xyz = jnp.where(row4 == 0, x, jnp.where(row4 == 1, y, z))
@@ -181,8 +194,8 @@
 
         def tile(m, total):
             p = partners[b, m]
-            part_pred = partner_rows(wide_pred, p)
-            part = jnp.concatenate([part_pred, partner_rows(wide_true, p)], axis=0).astype(bf16)
+            part_pred = partner_rows(wide_pred, p, 3)
+            part = jnp.concatenate([part_pred, partner_rows(wide_true, p, 4)], axis=0).astype(bf16)
             squares = dot(part, own, ((0,), (0,)))
             sp, st = squares[:, :PAIR_BLK], squares[:, PAIR_BLK:]
             rp = lax.rsqrt(sp)
@@ -200,12 +213,196 @@
 
         total = lax.fori_loop(0, counts[b], tile, jnp.zeros((8, PAIR_BLK), f32))
         for d, (pc, tc) in enumerate(((px, tx), (py, ty), (pz, tz))):
-            lg = scal[0] * (pc * total[4:5] - total[d : d + 1])
+            lg = pair_scale * (pc * total[4:5] - total[d : d + 1])
             lddt_grad[0, d : d + 1, at] = lg
-            coord_grad[0, d : d + 1, at] = scal[1] * (pc - tc) - lg * (1.0 / PAIR_BLK)
+            coord_grad[0, d : d + 1, at] = scal[0] * (pc - tc) - lg * (1.0 / PAIR_BLK)
         return 0
 
     lax.fori_loop(0, blocks, visit, 0)
+
+
+MESH = pl.DeviceIdType.MESH
+
+
+def remote(src, dst, send, recv, atom, sample):
+    return pltpu.make_async_remote_copy(
+        src_ref=src, dst_ref=dst, send_sem=send, recv_sem=recv,
+        device_id=(atom, sample), device_id_type=MESH,
+    )
+
+
+def share_kernel(
+    atom_peers, sample_peers, sigma, feats, proj, single, token, true, noise, counts,
+    tok, single_ext, cx, gathered,
+    partial, arrived, slab, pay, wide,
+    part_send, part_recv, tok_send, tok_recv, edge_send, edge_recv, near_send, near_recv,
+    all_send, all_recv, own_sem,
+):
+    me = lax.axis_index("atoms")
+    mine = lax.axis_index("samples")
+    right = lax.rem(me + 1, atom_peers)
+    left = lax.rem(me + atom_peers - 1, atom_peers)
+    rows = single.shape[0]
+    share = feats.shape[0] // sample_peers
+    pay_rows = pay.shape[0]
+
+    barrier = pltpu.get_barrier_semaphore()
+
+    def greet(atom, sample):
+        pl.semaphore_signal(barrier, inc=1, device_id=(atom, sample), device_id_type=MESH)
+
+    for step in range(1, sample_peers):
+        greet(me, lax.rem(mine + step, sample_peers))
+    for step in range(sample_peers):
+        greet(left, lax.rem(mine + step, sample_peers))
+        greet(right, lax.rem(mine + step, sample_peers))
+
+    @pl.loop(2, atom_peers - 1)
+    def _(step):
+        greet(lax.rem(me + step, atom_peers), mine)
+
+    own_copy = pltpu.make_async_copy(single, single_ext.at[pl.ds(HALO, rows)], own_sem)
+    own_copy.start()
+    partial[...] = dot(feats[...], proj[...])
+    inv = lax.rsqrt(jnp.full((8, 128), sigma[0] * sigma[0] + 4.0, f32))[0:1, 0:1]
+    cx[3:8, pl.ds(HALO, rows)] = jnp.concatenate(
+        [token[...].astype(f32), jnp.zeros((4, rows), f32)], axis=0
+    )
+    cx[0:3, pl.ds(HALO, rows)] = (true[...] + sigma[0] * noise[0]) * inv
+    blocks = rows // PAIR_BLK
+    for d in range(3):
+        for b in range(blocks):
+            wide[d * blocks + b : d * blocks + b + 1, :] = true[
+                d : d + 1, b * PAIR_BLK : (b + 1) * PAIR_BLK
+            ]
+    wide[3 * blocks : 4 * blocks, :] = jnp.broadcast_to(counts[...].astype(f32), (blocks, PAIR_BLK))
+    pay[...] = wide[...].astype(bf16)
+    gathered[pl.ds(pl.multiple_of(me * pay_rows, pay_rows), pay_rows), :] = pay[...]
+    pl.semaphore_wait(barrier, 7 + 2 * sample_peers + atom_peers - 3)
+
+    def part_copy(step):
+        peer = lax.rem(mine + step, sample_peers)
+        at = pl.multiple_of(peer * share, share)
+        return remote(
+            partial.at[pl.ds(at, share)], arrived.at[step], part_send.at[step], part_recv.at[step],
+            me, peer,
+        )
+
+    parts = [part_copy(step) for step in range(1, sample_peers)]
+    for copy in parts:
+        copy.start()
+    near = [
+        remote(single.at[pl.ds(rows - HALO, HALO)], single_ext.at[pl.ds(0, HALO)],
+               near_send.at[0], near_recv.at[0], right, mine),
+        remote(single.at[pl.ds(0, HALO)], single_ext.at[pl.ds(rows + HALO, HALO)],
+               near_send.at[1], near_recv.at[1], left, mine),
+        remote(cx.at[:, pl.ds(rows, HALO)], cx.at[:, pl.ds(0, HALO)],
+               near_send.at[2], near_recv.at[2], right, mine),
+        remote(cx.at[:, pl.ds(HALO, HALO)], cx.at[:, pl.ds(rows + HALO, HALO)],
+               near_send.at[3], near_recv.at[3], left, mine),
+    ]
+    for copy in near:
+        copy.start()
+    for copy in parts:
+        copy.wait_recv()
+    total = partial[pl.ds(pl.multiple_of(mine * share, share), share), :]
+    for step in range(1, sample_peers):
+        total = total + arrived[step]
+    slab[...] = total.astype(bf16)
+    my_rows = pl.ds(pl.multiple_of(TOK_HALO + mine * share, 16), share)
+    tok[my_rows, :] = slab[...]
+
+    def tok_copy(step):
+        return remote(
+            slab, tok.at[my_rows], tok_send.at[step], tok_recv.at[step],
+            me, lax.rem(mine + step, sample_peers),
+        )
+
+    toks = [tok_copy(step) for step in range(1, sample_peers)]
+    for copy in toks:
+        copy.start()
+    tokens = tok.shape[0] - 2 * TOK_HALO
+    half = TOK_HALO - share
+    edges = (
+        (sample_peers - 1, pl.ds(0, share), pl.ds(half, share), right),
+        (sample_peers - 2, pl.ds(share - half, half), pl.ds(0, half), right),
+        (0, pl.ds(0, share), pl.ds(TOK_HALO + tokens, share), left),
+        (1, pl.ds(0, half), pl.ds(TOK_HALO + tokens + share, half), left),
+    )
+
+    def edge_copy(i, step):
+        _, src, dst, to = edges[i]
+        return remote(
+            slab.at[src], tok.at[dst], edge_send.at[step], edge_recv.at[i],
+            to, lax.rem(mine + step, sample_peers),
+        )
+
+    for i, edge in enumerate(edges):
+        @pl.when(mine == edge[0])
+        def _(i=i):
+            for step in range(sample_peers):
+                edge_copy(i, step).start()
+
+    def all_copy(step):
+        at = pl.ds(pl.multiple_of(me * pay_rows, pay_rows), pay_rows)
+        return remote(
+            pay, gathered.at[at], all_send.at[step], all_recv.at[step],
+            lax.rem(me + step, atom_peers), mine,
+        )
+
+    @pl.loop(1, atom_peers)
+    def _(step):
+        all_copy(step).start()
+
+    for copy in parts:
+        copy.wait_send()
+    for copy in near:
+        copy.wait()
+    for copy in toks:
+        copy.wait()
+    for i, edge in enumerate(edges):
+        edge_copy(i, 0).wait_recv()
+
+        @pl.when(mine == edge[0])
+        def _(i=i):
+            for step in range(sample_peers):
+                edge_copy(i, step).wait_send()
+
+    @pl.loop(1, atom_peers)
+    def _(step):
+        all_copy(step).wait()
+
+    own_copy.wait()
+
+
+def spread_kernel(atom_peers, pay, gathered, send, recv):
+    me = lax.axis_index("atoms")
+    mine = lax.axis_index("samples")
+    rows = pay.shape[0]
+    barrier = pltpu.get_barrier_semaphore()
+
+    @pl.loop(1, atom_peers)
+    def _(step):
+        pl.semaphore_signal(
+            barrier, inc=1, device_id=(lax.rem(me + step, atom_peers), mine), device_id_type=MESH
+        )
+
+    at = pl.ds(pl.multiple_of(me * rows, rows), rows)
+    gathered[at, :] = pay[...]
+    pl.semaphore_wait(barrier, atom_peers - 1)
+
+    def copy(step):
+        return remote(
+            pay, gathered.at[at], send.at[step], recv.at[step], lax.rem(me + step, atom_peers), mine
+        )
+
+    @pl.loop(1, atom_peers)
+    def _(step):
+        copy(step).start()
+
+    @pl.loop(1, atom_peers)
+    def _(step):
+        copy(step).wait()
 
 
 def vmem(n):
@@ -230,13 +427,17 @@
     return pl.pallas_call(
         atoms_kernel,
         name="atoms",
-        out_shape=jax.ShapeDtypeStruct((8, rows), f32),
+        out_shape=(
+            jax.ShapeDtypeStruct((8, rows), f32),
+            jax.ShapeDtypeStruct((3 * (rows // PAIR_BLK), PAIR_BLK), bf16),
+        ),
         in_specs=smem(2) + vmem(10),
-        out_specs=pl.BlockSpec(memory_space=pltpu.VMEM),
+        out_specs=tuple(vmem(2)),
         scratch_shapes=[
             pltpu.VMEM((ext, CHANNELS), f32),
             pltpu.VMEM((2, ext, 3 * CHANNELS), bf16),
             pltpu.VMEM((ext, CHANNELS), f32),
+            pltpu.VMEM((3 * (rows // PAIR_BLK), PAIR_BLK), f32),
         ],
         compiler_params=pltpu.CompilerParams(vmem_limit_bytes=VMEM_LIMIT),
     )(place, scal, single, cx, tok, coord_w, w_qkv, w_o, w_gu, w_down, gains8, wout8)
@@ -244,7 +445,7 @@
 
 def run_pairs(scal, counts, partners, gathered_pred, gathered_true, pred, true):
     rows = pred.shape[1]
-    wide = pltpu.VMEM(gathered_pred.shape, f32)
+    wides = [pltpu.VMEM(g.shape, f32) for g in (gathered_pred, gathered_true)]
     out = jax.ShapeDtypeStruct((1, 3, rows), f32)
     return pl.pallas_call(
         pairs_kernel,
@@ -252,20 +453,58 @@
         out_shape=(out, out),
         in_specs=smem(3) + vmem(4),
         out_specs=tuple(vmem(2)),
-        scratch_shapes=[wide, wide],
+        scratch_shapes=wides,
         compiler_params=pltpu.CompilerParams(vmem_limit_bytes=VMEM_LIMIT),
     )(scal, counts, partners, gathered_pred, gathered_true, pred, true)
 
 
-def extended(value, axis, dim, width):
-    peers, length = (lax.axis_size(axis), value.shape[dim])
-    up = [(i, (i + 1) % peers) for i in range(peers)]
-    down = [(j, i) for i, j in up]
-    last = lax.slice_in_dim(value, length - width, length, axis=dim)
-    first = lax.slice_in_dim(value, 0, width, axis=dim)
-    before = lax.ppermute(last, axis, up)
-    after = lax.ppermute(first, axis, down)
-    return jnp.concatenate([before, value, after], axis=dim)
+def share(sigma, feats, proj, single, token, true, noise, counts):
+    atom_peers, sample_peers = lax.axis_size("atoms"), lax.axis_size("samples")
+    rows, tokens = single.shape[0], feats.shape[0]
+    blocks = rows // PAIR_BLK
+    part = tokens // sample_peers
+    dma = pltpu.SemaphoreType.DMA
+    return pl.pallas_call(
+        functools.partial(share_kernel, atom_peers, sample_peers),
+        name="share",
+        out_shape=(
+            jax.ShapeDtypeStruct((tokens + 2 * TOK_HALO, CHANNELS), bf16),
+            jax.ShapeDtypeStruct((rows + 2 * HALO, CHANNELS), bf16),
+            jax.ShapeDtypeStruct((8, rows + 2 * HALO), f32),
+            jax.ShapeDtypeStruct((atom_peers * 4 * blocks, PAIR_BLK), bf16),
+        ),
+        in_specs=smem(1) + vmem(7),
+        out_specs=tuple(vmem(4)),
+        scratch_shapes=[
+            pltpu.VMEM((tokens, CHANNELS), f32),
+            pltpu.VMEM((sample_peers, part, CHANNELS), f32),
+            pltpu.VMEM((part, CHANNELS), bf16),
+            pltpu.VMEM((4 * blocks, PAIR_BLK), bf16),
+            pltpu.VMEM((4 * blocks, PAIR_BLK), f32),
+            dma((sample_peers,)), dma((sample_peers,)), dma((sample_peers,)), dma((sample_peers,)),
+            dma((sample_peers,)), dma((4,)), dma((4,)), dma((4,)),
+            dma((atom_peers,)), dma((atom_peers,)), dma,
+        ],
+        compiler_params=pltpu.CompilerParams(
+            collective_id=0, has_side_effects=True, vmem_limit_bytes=VMEM_LIMIT
+        ),
+    )(sigma, feats, proj, single, token, true, noise, counts)
+
+
+def spread(pay):
+    atom_peers = lax.axis_size("atoms")
+    dma = pltpu.SemaphoreType.DMA
+    return pl.pallas_call(
+        functools.partial(spread_kernel, atom_peers),
+        name="spread",
+        out_shape=jax.ShapeDtypeStruct((atom_peers * pay.shape[0], pay.shape[1]), pay.dtype),
+        in_specs=vmem(1),
+        out_specs=vmem(1)[0],
+        scratch_shapes=[dma((atom_peers,)), dma((atom_peers,))],
+        compiler_params=pltpu.CompilerParams(
+            collective_id=1, has_side_effects=True, vmem_limit_bytes=VMEM_LIMIT
+        ),
+    )(pay)
 
 
 def on_device(
@@ -273,36 +512,25 @@
     w_qkv, w_o, w_gu, w_down, gains, w_out, pair_blocks, pair_count,
 ):
     rank = lax.axis_index("atoms")
-    tok_rows = token_feats.shape[0]
     rows = atom_single.shape[0]
-    total_atoms = rows * lax.axis_size("atoms")
-    whole_feats = lax.all_gather(token_feats, "samples", axis=1, tiled=True)
-    whole_proj = lax.all_gather(proj_w, "samples", axis=0, tiled=True)
-    token_proj = jnp.dot(whole_feats, whole_proj, preferred_element_type=f32).astype(bf16)
-    tok = extended(token_proj, "atoms", 0, TOK_HALO)
-    single = extended(atom_single, "atoms", 0, HALO)
+    tok, single, cx, gathered_true = share(
+        sigma, token_feats, proj_w, atom_single, atom_token[None], true_coords, noise,
+        pair_count[:, None],
+    )
     sig = sigma[0]
     noise_total = sig * sig + 4.0
     root = jnp.sqrt(noise_total)
-    scaled = (true_coords + sig * noise[0]) / root
-    cx = jnp.concatenate(
-        [scaled, atom_token.astype(f32)[None], jnp.zeros((4, rows), f32)], axis=0
-    )
-    cx = extended(cx, "atoms", 1, HALO)
-    place = jnp.stack([rank * rows, jnp.int32(total_atoms), rank * tok_rows]).astype(jnp.int32)
+    place = jnp.stack(
+        [rank * rows, jnp.int32(rows * lax.axis_size("atoms")), rank * token_feats.shape[0]]
+    ).astype(jnp.int32)
     scal = jnp.stack([4.0 / root, 2.0 * sig / root])
-    pred = run_atoms(place, scal, single, cx, tok, coord_in, w_qkv, w_o, w_gu, w_down, gains, w_out)
-
-    def everyone(v):
-        return lax.all_gather(v[:3].astype(bf16).reshape(-1, PAIR_BLK), "atoms", axis=0, tiled=True)
-
-    total_count = lax.psum(jnp.sum(pair_count), "atoms").astype(f32)
-    pair_total = total_count * (PAIR_BLK * PAIR_BLK) - PAIR_BLK * (total_atoms // PAIR_BLK)
-    scal2 = jnp.stack(
-        [total_atoms * PAIR_BLK / pair_total * (-0.0625), 2.0 / 3.0 * noise_total / (2.0 * sig) ** 2]
-    )
+    pred, pay = run_atoms(
+        place, scal, single, cx, tok, coord_in, w_qkv, w_o, w_gu, w_down, gains, w_out
+    )
+    gathered_pred = spread(pay)
+    scal2 = (2.0 / 3.0 * noise_total / (2.0 * sig) ** 2)[None]
     return run_pairs(
-        scal2, pair_count, pair_blocks, everyone(pred), everyone(true_coords), pred, true_coords
+        scal2, pair_count, pair_blocks, gathered_pred, gathered_true, pred, true_coords
     )
 
 

time: 330 us -> 209 us (0.63)
  the two profiles are of different devices: /device:TPU:230 before, /device:TPU:6 now
where the time goes in v1:
time: 209 us
  Pallas kernels  198 us (95%)
  local copies, waits for them, and re-layouts  7.6 us (4%)
    pallas_call x1, Pallas kernels, run_atoms(): pl.pallas_call(atoms_kernel, name='atoms', out_shape=(jax.ShapeDtypeStruc...  85.8 us
    pallas_call x1, Pallas kernels, run_pairs(): pl.pallas_call(pairs_kernel, name='pairs', out_shape=(out, out), in_specs...  63.5 us
    pallas_call x1, Pallas kernels, share(): pl.pallas_call(functools.partial(share_kernel, atom_peers, sample_peers),...  31.5 us
    pallas_call x1, Pallas kernels, spread(): pl.pallas_call(functools.partial(spread_kernel, atom_peers), name='spread...  17.4 us

profile of v1, /device:TPU:6, one launch (start us, length us, event | category | flops | bytes accessed | tf_op | source)
XLA Modules:
  0.0 208.6 jit_solution(2312074002411339272)
XLA Ops:
  1.4 0.7 pad_maximum_fusion.scal
  2.1 0.0 copy-start.2
  2.1 1.5 copy.18.feats
  3.6 0.0 copy-done.2
  3.6 0.6 copy.19.noise
  4.2 0.0 copy-start.5
  4.2 0.7 copy-done.5
  4.9 0.7 copy.20.counts
  5.6 31.5 %share.1 = (bf16[352,128]{1,0:T(8,128)(2,1)}, bf16[2560,128]{1,0:T(8,128)(2,1)}, f32[8,2560]{1,0:T(8,128)}, bf16[2048,128]{1,0:T(8,128)(2,1)}) custom-call(f32[1]{0:T(128)S(6)} %copy.28.sigma, bf16[256,96]{1,0:T(8,128)(2,1)} %copy.18.feats, bf16[96,128]{1,0:T(8,128)(2,1)} %proj.1, bf16[2048,128]{1,0:T(8,128)(2,1)} %single.1, s32[1,2048]{1,0:T(1,128)} %bitcast.5, ...), custom_call_target="tpu_custom_call" | custom-call | tf_op jit(solution)/shard_map/share/pallas_call | solution.py:467
  37.1 0.0 copy-start
  37.1 0.6 pad_add_fusion.place
  37.6 0.1 copy-done
  37.8 0.0 copy-start.4
  37.8 0.7 copy-done.4
  38.5 0.0 copy-start.3
  38.5 0.0 copy-start.6
  38.5 0.6 pad.12.gains
  39.1 0.1 copy-done.6
  39.2 0.6 pad.13.wout
  39.8 0.0 copy-done.3
  39.8 85.8 %atoms.1 = (f32[8,2048]{1,0:T(8,128)}, bf16[48,128]{1,0:T(8,128)(2,1)}) custom-call(s32[3]{0:T(128)} %pad_add_fusion.place, f32[2]{0:T(128)} %pad_maximum_fusion.scal, bf16[2560,128]{1,0:T(8,128)(2,1)} %get-tuple-element.8.single, f32[8,2560]{1,0:T(8,128)} %get-tuple-element.9.cx, bf16[352,128]{1,0:T(8,128)(2,1)} %get-tuple-element.10.tok, ...), custom_call_target="tpu_custom_call" | custom-call | tf_op jit(solution)/shard_map/atoms/pallas_call | solution.py:427
  125.5 17.4 %spread.1.gathered_pred = bf16[1536,128]{1,0:T(8,128)(2,1)} custom-call(bf16[48,128]{1,0:T(8,128)(2,1)} %get-tuple-element.11.pay), custom_call_target="tpu_custom_call" | custom-call | tf_op jit(solution)/shard_map/spread/pallas_call | solution.py:497
  143.0 63.5 %pairs.1 = (f32[1,3,2048]{2,1,0:T(4,128)}, f32[1,3,2048]{2,1,0:T(4,128)}) custom-call(f32[1]{0:T(128)S(6)} %div.12.scal, s32[16]{0:T(128)} %counts.1, s32[16,13]{1,0:T(8,128)} %partners.1, bf16[1536,128]{1,0:T(8,128)(2,1)} %spread.1.gathered_pred, bf16[2048,128]{1,0:T(8,128)(2,1)} %get-tuple-element.12.gathered_true, f32[8,2048]{1,0:T(8,128)} %get-tuple-element.13.pred, ...), custom_call_target="tpu_custom_call" | custom-call | tf_op jit(solution)/shard_map/pairs/pallas_call | solution.py:450
  206.5 0.0 copy-start.1
  206.5 1.4 copy.21
  207.9 0.0 copy-done.1
  207.9 0.6 copy.22
  (7 shorter events, 0.1 us)
Async XLA Ops:
  2.1 1.5 copy-start.2
  4.2 0.7 copy-start.5
  37.1 0.7 copy-start
  37.8 0.7 copy-start.4
  38.5 1.3 copy-start.3
  38.5 0.7 copy-start.6
  206.5 1.4 copy-start.1

commit v2 on v1

--- a/solution.py
+++ b/solution.py
@@ -17,6 +17,10 @@
 PAIR_BLK = 128
 CHANNELS = 128
 CHUNK = 256
+SIZE = 768
+SIZE_LAST = 1024
+FIRST_UNROLL = 5
+UNROLL = 8
 HALO = 256
 TOK_HALO = 48
 TOK_WIN = 64
@@ -43,14 +47,20 @@
 
 
 def atoms_kernel(
-    place, scal, single, cx, tok, coord_w, wqkv, wo, wgu, wdown, gains, wout,
-    pred, pay, hid, qkv, bias, wide,
+    place, sigma, single, cx, tok, coord_in, wqkv, wo, wgu, wdown, gains, wout,
+    pred, pay, hid, kv, queries, bias, wide,
 ):
     rows = single.shape[0] - 2 * HALO
     ext = single.shape[0]
     first_atom = place[0]
     total_atoms = place[1]
     first_tok = place[2]
+    sig = sigma[0]
+    inv = lax.rsqrt(jnp.full((8, CHANNELS), sig * sig + 4.0, f32))[0:1, 0:1]
+    zero5 = jnp.zeros((5, CHANNELS), f32)
+    hi, mid, lo = pieces(jnp.concatenate([coord_in[...], zero5], axis=0))
+    coord_w = jnp.concatenate([hi, mid, lo, hi, mid, hi], axis=0).astype(bf16)
+    head = jnp.concatenate([wout[...], zero5], axis=0)
     q_scale = math.log2(math.e) / math.sqrt(HEAD_DIM)
     lane = lax.broadcasted_iota(jnp.int32, (1, CHANNELS), 1) // HEAD_DIM
 
@@ -58,11 +68,22 @@
     bias[...] = jnp.where((pos >= 0) & (pos < total_atoms), 0.0, -1e30)
 
     def project(layer, at, h):
-        normed = (rms_scale(h) * gains[2 * layer : 2 * layer + 1, :]).astype(bf16)
+        normed = (rms_scale(h) * gains[layer, 0:1, :]).astype(bf16)
         out = dot(normed, wqkv[layer])
         rows_at = pl.ds(at, h.shape[0])
-        qkv[layer % 2, rows_at, 0:128] = (out[:, :128] * q_scale).astype(bf16)
-        qkv[layer % 2, rows_at, 128:384] = out[:, 128:].astype(bf16)
+        kv[layer % 2, rows_at, :] = out[:, 128:].astype(bf16)
+        for t in range(h.shape[0] // CHANNELS):
+            turned = (out[t * CHANNELS : (t + 1) * CHANNELS, :128] * q_scale).T
+            shifted = [turned if r == 0 else pltpu.roll(turned, r * QBLK, 1) for r in range(HEADS)]
+            for w in range(CHANNELS // QBLK):
+                spread = jnp.concatenate(
+                    [
+                        jnp.where(lane == h, shifted[(h - w) % HEADS][h * QBLK : (h + 1) * QBLK], 0.0)
+                        for h in range(HEADS)
+                    ],
+                    axis=0,
+                )
+                queries[layer % 2, at // QBLK + t * HEADS + w] = spread.astype(bf16)
 
     def first(k, _):
         at = pl.multiple_of(k * CHUNK, CHUNK)
@@ -72,25 +93,22 @@
         hot = jnp.where(lax.broadcasted_iota(jnp.int32, (TOK_WIN, CHUNK), 0) == rel, 1.0, 0.0)
         left = jnp.concatenate([hot, hi, hi, hi, mid, mid, lo], axis=0).astype(bf16)
         tok_at = pl.ds(pl.multiple_of(k * (CHUNK // 8), CHUNK // 8), TOK_WIN)
-        right = jnp.concatenate([tok[tok_at, :], coord_w[...]], axis=0)
+        right = jnp.concatenate([tok[tok_at, :], coord_w], axis=0)
         h = single[pl.ds(at, CHUNK), :].astype(f32) + dot(left, right, ((0,), (0,)))
         hid[pl.ds(at, CHUNK), :] = h
         project(0, at, h)
         return 0
 
-    lax.fori_loop(0, ext // CHUNK, first, 0)
+    lax.fori_loop(0, ext // CHUNK, first, 0, unroll=FIRST_UNROLL)
 
     def attend(layer, at, size):
         buf = layer % 2
         outs = []
         for w in range(size // QBLK):
-            q = qkv[buf, pl.ds(at + w * QBLK, QBLK), 0:128]
             keys_at = pl.ds(at + (w * QBLK - 48), KWIN)
-            keys = qkv[buf, keys_at, 128:256]
-            values = qkv[buf, keys_at, 256:384]
-            zero = jnp.zeros_like(q)
-            spread = jnp.concatenate([jnp.where(lane == h, q, zero) for h in range(HEADS)], axis=0)
-            scores = dot(keys, spread, ((1,), (1,))) + bias[keys_at, :]
+            keys = kv[buf, keys_at, 0:128]
+            values = kv[buf, keys_at, 128:256]
+            scores = dot(keys, queries[buf, at // QBLK + w]) + bias[keys_at, :]
             top = jnp.max(scores, axis=0, keepdims=True)
             weights = jnp.exp2(scores - top)
             weights = (weights * (1.0 / jnp.sum(weights, axis=0, keepdims=True))).astype(bf16)
@@ -104,7 +122,7 @@
     def block(layer, at, size):
         h = hid[pl.ds(at, size), :]
         h = h + dot(attend(layer, at, size), wo[layer])
-        normed = (rms_scale(h) * gains[2 * layer + 1 : 2 * layer + 2, :]).astype(bf16)
+        normed = (rms_scale(h) * gains[layer, 1:2, :]).astype(bf16)
         gu = dot(normed, wgu[layer])
         half = 0.5 * gu[:, :FF_ATOM]
         inner = (half * (1.0 + jnp.tanh(half)) * gu[:, FF_ATOM:]).astype(bf16)
@@ -113,10 +131,10 @@
             hid[pl.ds(at, size), :] = h
             project(layer + 1, at, h)
         else:
-            update = dot(wout[...], rms_scale(h), ((1,), (1,)), lax.Precision.HIGHEST)
+            update = dot(head, rms_scale(h), ((1,), (1,)), lax.Precision.HIGHEST)
             noisy = cx[:, pl.ds(at, size)]
-            out = scal[0] * noisy + scal[1] * update
-            pred[:, pl.ds(pl.multiple_of(at - HALO, size), size)] = out
+            out = inv * (4.0 * noisy + (2.0 * sig) * update)
+            pred[:, pl.ds(pl.multiple_of(at - HALO, 128), size)] = out
             first_block = (at - HALO) // PAIR_BLK
             for i in range(size // PAIR_BLK):
                 for d in range(3):
@@ -126,18 +144,19 @@
     for layer in range(LAYERS):
         low = HALO if layer == LAYERS - 1 else HALO - 128
         span = rows if layer == LAYERS - 1 else rows + 256
-
-        def step(k, _, layer=layer, low=low):
-            block(layer, pl.multiple_of(low + k * CHUNK, 128), CHUNK)
+        size = SIZE_LAST if layer == LAYERS - 1 else SIZE
+
+        def step(k, _, layer=layer, low=low, size=size):
+            block(layer, pl.multiple_of(low + k * size, 128), size)
             return 0
 
-        lax.fori_loop(0, span // CHUNK, step, 0)
+        lax.fori_loop(0, span // size, step, 0)
     pay[...] = wide[...].astype(bf16)
 
 
 def pairs_kernel(
-    scal, counts, partners, gathered_pred, gathered_true, pred, true,
-    coord_grad, lddt_grad, wide_pred, wide_true,
+    sigma, counts, partners, gathered_pred, gathered_true, pred, true,
+    coord_grad, lddt_grad, wide_pred, wide_true, owns, totals,
 ):
     blocks = counts.shape[0]
     wide_pred[...] = gathered_pred[...].astype(f32)
@@ -155,19 +174,21 @@
         jnp.int32, (PAIR_BLK, PAIR_BLK), 1
     )
 
-    def partner_rows(wide, p, per):
-        base = p // blocks * (per * blocks) + p % blocks
-        x, y, z = (wide[pl.ds(base + d * blocks, 1), :] for d in range(3))
+    def partner_rows(p):
+        base = p // blocks * (4 * blocks) + p % blocks
+        x, y, z = (wide_true[pl.ds(base + d * blocks, 1), :] for d in range(3))
         n1, n2, n3 = pieces(x * x + y * y + z * z)
         xyz = jnp.where(row4 == 0, x, jnp.where(row4 == 1, y, z))
         upper = jnp.where(row4 == 3, jnp.where(row8 == 3, n1, n2), xyz)
         ones = jnp.where(row8 < 7, 1.0, 0.0)
         lower = jnp.where(row8 < 3, xyz, jnp.where(row8 == 3, n3, ones))
-        return jnp.concatenate([upper, lower], axis=0)
-
-    def own_rows(x, y, z):
-        n = x * x + y * y + z * z + 1.0
-        n1, n2, n3 = pieces(0.25 * n)
+        base = p // blocks * (3 * blocks) + p % blocks
+        x, y, z = (wide_pred[pl.ds(base + d * blocks, 1), :] for d in range(3))
+        xyz = jnp.where(row8 == 0, x, jnp.where(row8 == 1, y, jnp.where(row8 == 2, z, 0.0)))
+        return jnp.concatenate([upper, lower, xyz, jnp.zeros_like(xyz)], axis=0).astype(bf16)
+
+    def own_square(x, y, z):
+        n1, n2, n3 = pieces(0.25 * (x * x + y * y + z * z + 1.0))
         xp, yp, zp = pieces(-0.5 * x), pieces(-0.5 * y), pieces(-0.5 * z)
 
         def xyz(i):
@@ -177,48 +198,74 @@
         norms = jnp.where(row8 == 4, n1, jnp.where(row8 == 5, n2, n3))
         norms = jnp.where(row8 == 7, 0.0, norms)
         lower = jnp.where(row8 < 3, xyz(2), jnp.where(row8 == 3, 0.25, norms))
-        return jnp.concatenate([upper, lower], axis=0)
-
-    def visit(b, _):
-        at = pl.ds(pl.multiple_of(b * PAIR_BLK, PAIR_BLK), PAIR_BLK)
-        px, py, pz = (pred[d : d + 1, at] for d in range(3))
-        tx, ty, tz = (true[d : d + 1, at] for d in range(3))
-        none = jnp.zeros((16, PAIR_BLK), f32)
-        own = jnp.concatenate(
-            [
-                jnp.concatenate([own_rows(px, py, pz), none], axis=1),
-                jnp.concatenate([none, own_rows(tx, ty, tz)], axis=1),
-            ],
-            axis=0,
+        zero = jnp.zeros_like(lower)
+        return jnp.concatenate([upper, lower, zero, zero], axis=0)
+
+    def own_gap(d, x):
+        hi, mid, lo = pieces(-0.5 * x)
+        zero = jnp.zeros((8, PAIR_BLK), f32)
+        lower = jnp.where(row8 == 4, hi, jnp.where(row8 == 5, mid, jnp.where(row8 == 6, lo, 0.0)))
+        pick = jnp.where(row8 == d, 0.5, 0.0)
+        return jnp.concatenate([zero, lower, pick, zero], axis=0)
+
+    square = sigma[0] * sigma[0]
+    mse_scale = jnp.full((1, PAIR_BLK), square + 4.0, f32) / jnp.full((1, PAIR_BLK), 6.0 * square, f32)
+    totals[...] = jnp.zeros_like(totals)
+    owns[blocks] = jnp.zeros(owns.shape[1:], bf16) + 1.0
+    for b in range(blocks):
+        at = slice(b * PAIR_BLK, (b + 1) * PAIR_BLK)
+        owns[b] = jnp.concatenate(
+            [own_square(*(true[d : d + 1, at] for d in range(3)))]
+            + [own_gap(d, pred[d : d + 1, at]) for d in range(3)],
+            axis=1,
         ).astype(bf16)
 
-        def tile(m, total):
-            p = partners[b, m]
-            part_pred = partner_rows(wide_pred, p, 3)
-            part = jnp.concatenate([part_pred, partner_rows(wide_true, p, 4)], axis=0).astype(bf16)
-            squares = dot(part, own, ((0,), (0,)))
-            sp, st = squares[:, :PAIR_BLK], squares[:, PAIR_BLK:]
-            rp = lax.rsqrt(sp)
-            gap = sp * rp - st * lax.rsqrt(st)
-            e2 = gap * gap + 0.0025
-            re = lax.rsqrt(e2)
-            err = e2 * re
-            th = [jnp.tanh(0.5 * t - err) for t in (0.5, 1.0, 2.0, 4.0)]
-            slope = 4.0 - (th[0] * th[0] + th[1] * th[1] + th[2] * th[2] + th[3] * th[3])
-            coef = slope * gap * (re * rp)
-            shut = jnp.where(m == 0, 0, 2 * PAIR_BLK)
-            coef = jnp.where(diff == shut, 0.0, coef)
-            sums = dot(part[0:16], coef.astype(bf16))
-            return total + sums[8:16]
-
-        total = lax.fori_loop(0, counts[b], tile, jnp.zeros((8, PAIR_BLK), f32))
-        for d, (pc, tc) in enumerate(((px, tx), (py, ty), (pz, tz))):
-            lg = pair_scale * (pc * total[4:5] - total[d : d + 1])
-            lddt_grad[0, d : d + 1, at] = lg
-            coord_grad[0, d : d + 1, at] = scal[0] * (pc - tc) - lg * (1.0 / PAIR_BLK)
-        return 0
-
-    lax.fori_loop(0, blocks, visit, 0)
+    def tile(b, m):
+        known = jnp.minimum(b, blocks - 1)
+        p = partners[known, m]
+        found = dot(partner_rows(p), owns[b], ((0,), (0,)))
+        st, gx, gy, gz = (found[:, i * PAIR_BLK : (i + 1) * PAIR_BLK] for i in range(4))
+        sp = gx * gx + gy * gy + gz * gz + 0.25
+        rp = lax.rsqrt(sp)
+        gap = sp * rp - st * lax.rsqrt(st)
+        e2 = gap * gap + 0.0025
+        re = lax.rsqrt(e2)
+        err = e2 * re
+        th = [jnp.tanh(0.5 * t - err) for t in (0.5, 1.0, 2.0, 4.0)]
+        slope = 4.0 - (th[0] * th[0] + th[1] * th[1] + th[2] * th[2] + th[3] * th[3])
+        coef = slope * gap * (re * rp)
+        shut = jnp.where(m == 0, 0, 2 * PAIR_BLK)
+        coef = jnp.where(diff == shut, 0.0, coef)
+        sums = jnp.concatenate(
+            [jnp.sum((coef * g).reshape(16, 8, PAIR_BLK), axis=0) for g in (gx, gy, gz)], axis=0
+        )
+        last = m + 1 >= counts[known]
+        return sums, jnp.where(last, jnp.minimum(b + 1, blocks), b), jnp.where(last, 0, m + 1)
+
+    def visit(_, place):
+        b, m = place
+        found = []
+        for _ in range(UNROLL):
+            sums, after, then = tile(b, m)
+            found.append((b, sums))
+            b, m = after, then
+        for at, sums in found:
+            totals[at] = totals[at] + sums
+        return b, m
+
+    live = counts[0]
+    for b in range(1, blocks):
+        live = live + counts[b]
+    lax.fori_loop(0, (live + UNROLL - 1) // UNROLL, visit, (jnp.int32(0), jnp.int32(0)))
+
+    for b in range(blocks):
+        at = slice(b * PAIR_BLK, (b + 1) * PAIR_BLK)
+        total = totals[b]
+        for d in range(3):
+            pc, tc = pred[d : d + 1, at], true[d : d + 1, at]
+            lg = (-2.0 * pair_scale) * jnp.sum(total[8 * d : 8 * d + 8], axis=0, keepdims=True)
+            lddt_grad[d, :, at] = lg
+            coord_grad[d, :, at] = mse_scale * (pc - tc) - lg * (1.0 / PAIR_BLK)
 
 
 MESH = pl.DeviceIdType.MESH
@@ -232,7 +279,7 @@
 
 
 def share_kernel(
-    atom_peers, sample_peers, sigma, feats, proj, single, token, true, noise, counts,
+    atom_peers, sample_peers, sigma, counts, feats, proj, single, token, true, noise,
     tok, single_ext, cx, gathered,
     partial, arrived, slab, pay, wide,
     part_send, part_recv, tok_send, tok_recv, edge_send, edge_recv, near_send, near_recv,
@@ -243,7 +290,7 @@
     right = lax.rem(me + 1, atom_peers)
     left = lax.rem(me + atom_peers - 1, atom_peers)
     rows = single.shape[0]
-    share = feats.shape[0] // sample_peers
+    share = feats.shape[1] // sample_peers
     pay_rows = pay.shape[0]
 
     barrier = pltpu.get_barrier_semaphore()
@@ -263,19 +310,21 @@
 
     own_copy = pltpu.make_async_copy(single, single_ext.at[pl.ds(HALO, rows)], own_sem)
     own_copy.start()
-    partial[...] = dot(feats[...], proj[...])
+    partial[...] = dot(feats[...], proj[...], ((0,), (0,)))
     inv = lax.rsqrt(jnp.full((8, 128), sigma[0] * sigma[0] + 4.0, f32))[0:1, 0:1]
     cx[3:8, pl.ds(HALO, rows)] = jnp.concatenate(
         [token[...].astype(f32), jnp.zeros((4, rows), f32)], axis=0
     )
-    cx[0:3, pl.ds(HALO, rows)] = (true[...] + sigma[0] * noise[0]) * inv
+    for d in range(3):
+        cx[d : d + 1, pl.ds(HALO, rows)] = (true[d : d + 1, :] + sigma[0] * noise[d]) * inv
     blocks = rows // PAIR_BLK
     for d in range(3):
         for b in range(blocks):
             wide[d * blocks + b : d * blocks + b + 1, :] = true[
                 d : d + 1, b * PAIR_BLK : (b + 1) * PAIR_BLK
             ]
-    wide[3 * blocks : 4 * blocks, :] = jnp.broadcast_to(counts[...].astype(f32), (blocks, PAIR_BLK))
+    for b in range(blocks):
+        wide[3 * blocks + b : 3 * blocks + b + 1, :] = jnp.full((1, PAIR_BLK), counts[b], jnp.int32).astype(f32)
     pay[...] = wide[...].astype(bf16)
     gathered[pl.ds(pl.multiple_of(me * pay_rows, pay_rows), pay_rows), :] = pay[...]
     pl.semaphore_wait(barrier, 7 + 2 * sample_peers + atom_peers - 3)
@@ -413,17 +462,9 @@
     return [pl.BlockSpec(memory_space=pltpu.SMEM)] * n
 
 
-def run_atoms(place, scal, single, cx, tok, coord_in, w_qkv, w_o, w_gu, w_down, gains, w_out):
+def run_atoms(place, sigma, single, cx, tok, coord_in, w_qkv, w_o, w_gu, w_down, gains, w_out):
     ext = single.shape[0]
     rows = ext - 2 * HALO
-    c3 = jnp.pad(coord_in, ((0, 5), (0, 0)))
-    hi, mid, lo = (lax.reduce_precision(c3, 8, 7), None, None)
-    rest = c3 - hi
-    mid = lax.reduce_precision(rest, 8, 7)
-    lo = rest - mid
-    coord_w = jnp.concatenate([hi, mid, lo, hi, mid, hi], axis=0).astype(bf16)
-    gains8 = jnp.pad(gains.reshape(2 * LAYERS, CHANNELS), ((0, 2), (0, 0)))
-    wout8 = jnp.pad(w_out.T, ((0, 5), (0, 0)))
     return pl.pallas_call(
         atoms_kernel,
         name="atoms",
@@ -435,32 +476,38 @@
         out_specs=tuple(vmem(2)),
         scratch_shapes=[
             pltpu.VMEM((ext, CHANNELS), f32),
-            pltpu.VMEM((2, ext, 3 * CHANNELS), bf16),
+            pltpu.VMEM((2, ext, 2 * CHANNELS), bf16),
+            pltpu.VMEM((2, ext // QBLK, CHANNELS, CHANNELS), bf16),
             pltpu.VMEM((ext, CHANNELS), f32),
             pltpu.VMEM((3 * (rows // PAIR_BLK), PAIR_BLK), f32),
         ],
         compiler_params=pltpu.CompilerParams(vmem_limit_bytes=VMEM_LIMIT),
-    )(place, scal, single, cx, tok, coord_w, w_qkv, w_o, w_gu, w_down, gains8, wout8)
-
-
-def run_pairs(scal, counts, partners, gathered_pred, gathered_true, pred, true):
+    )(place, sigma, single, cx, tok, coord_in, w_qkv, w_o, w_gu, w_down, gains, w_out.T)
+
+
+def run_pairs(sigma, counts, partners, gathered_pred, gathered_true, pred, true):
     rows = pred.shape[1]
     wides = [pltpu.VMEM(g.shape, f32) for g in (gathered_pred, gathered_true)]
-    out = jax.ShapeDtypeStruct((1, 3, rows), f32)
-    return pl.pallas_call(
+    out = jax.ShapeDtypeStruct((3, 1, rows), f32)
+    coord_grad, lddt_grad = pl.pallas_call(
         pairs_kernel,
         name="pairs",
         out_shape=(out, out),
         in_specs=smem(3) + vmem(4),
         out_specs=tuple(vmem(2)),
-        scratch_shapes=wides,
+        scratch_shapes=wides
+        + [
+            pltpu.VMEM((rows // PAIR_BLK + 1, 32, 4 * PAIR_BLK), bf16),
+            pltpu.VMEM((rows // PAIR_BLK + 1, 24, PAIR_BLK), f32),
+        ],
         compiler_params=pltpu.CompilerParams(vmem_limit_bytes=VMEM_LIMIT),
-    )(scal, counts, partners, gathered_pred, gathered_true, pred, true)
+    )(sigma, counts, partners, gathered_pred, gathered_true, pred, true)
+    return jnp.swapaxes(coord_grad, 0, 1), jnp.swapaxes(lddt_grad, 0, 1)
 
 
 def share(sigma, feats, proj, single, token, true, noise, counts):
     atom_peers, sample_peers = lax.axis_size("atoms"), lax.axis_size("samples")
-    rows, tokens = single.shape[0], feats.shape[0]
+    rows, tokens = single.shape[0], feats.shape[1]
     blocks = rows // PAIR_BLK
     part = tokens // sample_peers
     dma = pltpu.SemaphoreType.DMA
@@ -473,7 +520,7 @@
             jax.ShapeDtypeStruct((8, rows + 2 * HALO), f32),
             jax.ShapeDtypeStruct((atom_peers * 4 * blocks, PAIR_BLK), bf16),
         ),
-        in_specs=smem(1) + vmem(7),
+        in_specs=smem(2) + vmem(6),
         out_specs=tuple(vmem(4)),
         scratch_shapes=[
             pltpu.VMEM((tokens, CHANNELS), f32),
@@ -488,7 +535,7 @@
         compiler_params=pltpu.CompilerParams(
             collective_id=0, has_side_effects=True, vmem_limit_bytes=VMEM_LIMIT
         ),
-    )(sigma, feats, proj, single, token, true, noise, counts)
+    )(sigma, counts, feats, proj, single, token, true, noise)
 
 
 def spread(pay):
@@ -514,23 +561,18 @@
     rank = lax.axis_index("atoms")
     rows = atom_single.shape[0]
     tok, single, cx, gathered_true = share(
-        sigma, token_feats, proj_w, atom_single, atom_token[None], true_coords, noise,
-        pair_count[:, None],
-    )
-    sig = sigma[0]
-    noise_total = sig * sig + 4.0
-    root = jnp.sqrt(noise_total)
+        sigma, token_feats.T, proj_w, atom_single, atom_token[None], true_coords,
+        jnp.swapaxes(noise, 0, 1), pair_count,
+    )
     place = jnp.stack(
         [rank * rows, jnp.int32(rows * lax.axis_size("atoms")), rank * token_feats.shape[0]]
     ).astype(jnp.int32)
-    scal = jnp.stack([4.0 / root, 2.0 * sig / root])
     pred, pay = run_atoms(
-        place, scal, single, cx, tok, coord_in, w_qkv, w_o, w_gu, w_down, gains, w_out
+        place, sigma, single, cx, tok, coord_in, w_qkv, w_o, w_gu, w_down, gains, w_out
     )
     gathered_pred = spread(pay)
-    scal2 = (2.0 / 3.0 * noise_total / (2.0 * sig) ** 2)[None]
     return run_pairs(
-        scal2, pair_count, pair_blocks, gathered_pred, gathered_true, pred, true_coords
+        sigma, pair_count, pair_blocks, gathered_pred, gathered_true, pred, true_coords
     )
 
 

time: 209 us -> 95.4 us (0.46)
  the two profiles are of different devices: /device:TPU:6 before, /device:TPU:166 now
where the time goes in v2:
time: 95.4 us; the launch traced here: 95.1 us
  Pallas kernels  93.2 us (98%)
  between operations  1.3 us (1%)
    pallas_call x1, Pallas kernels, share(): pl.pallas_call(functools.partial(share_kernel, atom_peers, sample_peers),...  29.5 us
    pallas_call x1, Pallas kernels, run_pairs(): pl.pallas_call(pairs_kernel, name='pairs', out_shape=(out, out), in_specs...  23.8 us
    pallas_call x1, Pallas kernels, run_atoms(): pl.pallas_call(atoms_kernel, name='atoms', out_shape=(jax.ShapeDtypeStruc...  22.5 us
    pallas_call x1, Pallas kernels, spread(): pl.pallas_call(functools.partial(spread_kernel, atom_peers), name='spread...  17.6 us

profile of v2, /device:TPU:166, one launch (start us, length us, event | category | flops | bytes accessed | tf_op | source)
XLA Modules:
  0.0 95.1 jit_solution(11280627845960071938)
XLA Ops:
  1.3 0.6 pad_add_fusion.place
  1.9 29.5 %share.1 = (bf16[352,128]{1,0:T(8,128)(2,1)}, bf16[2560,128]{1,0:T(8,128)(2,1)}, f32[8,2560]{1,0:T(8,128)}, bf16[2048,128]{1,0:T(8,128)(2,1)}) custom-call(f32[1]{0:T(128)S(6)} %copy.18.sigma, s32[16]{0:T(128)} %counts.3, bf16[96,256]{1,0:T(8,128)(2,1)} %bitcast.8, bf16[96,128]{1,0:T(8,128)(2,1)} %proj.1, bf16[2048,128]{1,0:T(8,128)(2,1)} %single.1, ...), custom_call_target="tpu_custom_call" | custom-call | tf_op jit(solution)/shard_map/share/pallas_call | solution.py:514
  31.3 22.5 %atoms.1 = (f32[8,2048]{1,0:T(8,128)}, bf16[48,128]{1,0:T(8,128)(2,1)}) custom-call(s32[3]{0:T(128)} %pad_add_fusion.place, f32[1]{0:T(128)S(6)} %copy.18.sigma, bf16[2560,128]{1,0:T(8,128)(2,1)} %get-tuple-element.10.single, f32[8,2560]{1,0:T(8,128)} %get-tuple-element.11.cx, bf16[352,128]{1,0:T(8,128)(2,1)} %get-tuple-element.12.tok, f32[3,128]{1,0:T(4,128)} %coord_in.1, ...), custom_call_target="tpu_custom_call" | custom-call | tf_op jit(solution)/shard_map/atoms/pallas_call | solution.py:468
  53.8 17.6 %spread.1.gathered_pred = bf16[1536,128]{1,0:T(8,128)(2,1)} custom-call(bf16[48,128]{1,0:T(8,128)(2,1)} %get-tuple-element.13.pay), custom_call_target="tpu_custom_call" | custom-call | tf_op jit(solution)/shard_map/spread/pallas_call | solution.py:544
  71.4 23.8 %pairs.1 = (f32[3,1,2048]{2,1,0:T(1,128)}, f32[3,1,2048]{2,1,0:T(1,128)}) custom-call(f32[1]{0:T(128)S(6)} %copy.18.sigma, s32[16]{0:T(128)} %counts.3, s32[16,13]{1,0:T(8,128)} %partners.1, bf16[1536,128]{1,0:T(8,128)(2,1)} %spread.1.gathered_pred, bf16[2048,128]{1,0:T(8,128)(2,1)} %get-tuple-element.14.gathered_true, f32[8,2048]{1,0:T(8,128)} %get-tuple-element.15.pred, ...), custom_call_target="tpu_custom_call" | custom-call | tf_op jit(solution)/shard_map/pairs/pallas_call | solution.py:492

commit v3 on v2

--- a/solution.py
+++ b/solution.py
@@ -25,6 +25,7 @@
 TOK_HALO = 48
 TOK_WIN = 64
 EPS = 1e-05
+DEPTH = 8
 VMEM_LIMIT = 56 * 1024 * 1024
 
 f32 = jnp.float32
@@ -46,15 +47,109 @@
     return h * lax.rsqrt(jnp.mean(h * h, axis=1, keepdims=True) + EPS)
 
 
+MESH = pl.DeviceIdType.MESH
+
+
+def remote(src, dst, send, recv, atom, sample):
+    return pltpu.make_async_remote_copy(
+        src_ref=src, dst_ref=dst, send_sem=send, recv_sem=recv,
+        device_id=(atom, sample), device_id_type=MESH,
+    )
+
+def gather_plan(atom_peers):
+    nz = DEPTH
+    nx = atom_peers // nz
+    me = lax.axis_index("atoms")
+    x, z = me // nz, lax.rem(me, nz)
+
+    def along_z(dz):
+        return x * nz + lax.rem(z + dz + nz, nz)
+
+    def along_x(dx):
+        return lax.rem(x + dx, nx) * nz + z
+
+    return nz, nx, me, along_z, along_x
+
+
+class Gather:
+    def __init__(self, atom_peers, pay, whole, sems):
+        self.nz, self.nx, self.me, self.along_z, self.along_x = gather_plan(atom_peers)
+        self.mine = lax.axis_index("samples")
+        self.pay, self.whole = pay, whole
+        self.z_send, self.z_recv, self.x_send, self.x_recv = sems
+        self.order = [0]
+        for step in range(1, self.nz // 2 + 1):
+            self.order += [step, self.nz - step] if 2 * step != self.nz else [step]
+
+    def rows(self, owner):
+        size = self.pay.shape[0]
+        return pl.ds(pl.multiple_of(owner * size, size), size)
+
+    def z_copy(self, dz):
+        return remote(
+            self.pay, self.whole.at[self.rows(self.me)], self.z_send.at[dz], self.z_recv.at[dz],
+            self.along_z(dz), self.mine,
+        )
+
+    def x_copy(self, dz, dx):
+        at = self.rows(self.along_z(-dz))
+        src = self.pay if dz == 0 else self.whole.at[at]
+        slot = dz * self.nx + dx
+        return remote(
+            src, self.whole.at[at], self.x_send.at[slot], self.x_recv.at[slot],
+            self.along_x(dx), self.mine,
+        )
+
+    def start(self):
+        for dz in self.order[1:]:
+            self.z_copy(dz).start()
+        for dx in range(1, self.nx):
+            self.x_copy(0, dx).start()
+        self.whole[self.rows(self.me), :] = self.pay[...]
+
+    def forward(self):
+        for dz in self.order[1:]:
+            self.z_copy(dz).wait_recv()
+            for dx in range(1, self.nx):
+                self.x_copy(dz, dx).start()
+
+    def finish(self):
+        for dz in self.order[1:]:
+            self.z_copy(dz).wait_send()
+        for dz in self.order:
+            for dx in range(1, self.nx):
+                self.x_copy(dz, dx).wait()
+
+
 def atoms_kernel(
-    place, sigma, single, cx, tok, coord_in, wqkv, wo, wgu, wdown, gains, wout,
-    pred, pay, hid, kv, queries, bias, wide,
+    atom_peers, sigma, counts, true, single, cx, tok, coord_in, wqkv, wo, wgu, wdown, gains, wout,
+    pred, gathered_pred, gathered_true, hid, kv, queries, bias, pay, true_pay, wide, *sems,
 ):
     rows = single.shape[0] - 2 * HALO
     ext = single.shape[0]
-    first_atom = place[0]
-    total_atoms = place[1]
-    first_tok = place[2]
+    nz, nx, me, along_z, along_x = gather_plan(atom_peers)
+    mine = lax.axis_index("samples")
+    barrier = pltpu.get_barrier_semaphore()
+    for dz in range(1, nz):
+        pl.semaphore_signal(barrier, inc=1, device_id=(along_z(dz), mine), device_id_type=MESH)
+    for dx in range(1, nx):
+        pl.semaphore_signal(barrier, inc=1, device_id=(along_x(dx), mine), device_id_type=MESH)
+    first_atom = me * rows
+    total_atoms = rows * atom_peers
+    first_tok = me * (tok.shape[0] - 2 * TOK_HALO)
+    blocks = rows // PAIR_BLK
+    for d in range(3):
+        for b in range(blocks):
+            wide[d * blocks + b : d * blocks + b + 1, :] = true[
+                d : d + 1, b * PAIR_BLK : (b + 1) * PAIR_BLK
+            ]
+    for b in range(blocks):
+        wide[3 * blocks + b : 3 * blocks + b + 1, :] = jnp.full((1, PAIR_BLK), counts[b], jnp.int32).astype(f32)
+    true_pay[...] = wide[...].astype(bf16)
+    pl.semaphore_wait(barrier, nz + nx - 2)
+    true_gather = Gather(atom_peers, true_pay, gathered_true, sems[:4])
+    pred_gather = Gather(atom_peers, pay, gathered_pred, sems[4:])
+    true_gather.start()
     sig = sigma[0]
     inv = lax.rsqrt(jnp.full((8, CHANNELS), sig * sig + 4.0, f32))[0:1, 0:1]
     zero5 = jnp.zeros((5, CHANNELS), f32)
@@ -100,6 +195,8 @@
         return 0
 
     lax.fori_loop(0, ext // CHUNK, first, 0, unroll=FIRST_UNROLL)
+
+    true_gather.forward()
 
     def attend(layer, at, size):
         buf = layer % 2
@@ -151,7 +248,11 @@
             return 0
 
         lax.fori_loop(0, span // size, step, 0)
-    pay[...] = wide[...].astype(bf16)
+    pay[...] = wide[0 : 3 * blocks, :].astype(bf16)
+    pred_gather.start()
+    pred_gather.forward()
+    true_gather.finish()
+    pred_gather.finish()
 
 
 def pairs_kernel(
@@ -268,22 +369,11 @@
             coord_grad[d, :, at] = mse_scale * (pc - tc) - lg * (1.0 / PAIR_BLK)
 
 
-MESH = pl.DeviceIdType.MESH
-
-
-def remote(src, dst, send, recv, atom, sample):
-    return pltpu.make_async_remote_copy(
-        src_ref=src, dst_ref=dst, send_sem=send, recv_sem=recv,
-        device_id=(atom, sample), device_id_type=MESH,
-    )
-
-
 def share_kernel(
-    atom_peers, sample_peers, sigma, counts, feats, proj, single, token, true, noise,
-    tok, single_ext, cx, gathered,
-    partial, arrived, slab, pay, wide,
-    part_send, part_recv, tok_send, tok_recv, edge_send, edge_recv, near_send, near_recv,
-    all_send, all_recv, own_sem,
+    atom_peers, sample_peers, sigma, feats, proj, single, token, true, noise,
+    tok, single_ext, cx,
+    partial, arrived, slab,
+    part_send, part_recv, tok_send, tok_recv, edge_send, edge_recv, near_send, near_recv, own_sem,
 ):
     me = lax.axis_index("atoms")
     mine = lax.axis_index("samples")
@@ -291,7 +381,6 @@
     left = lax.rem(me + atom_peers - 1, atom_peers)
     rows = single.shape[0]
     share = feats.shape[1] // sample_peers
-    pay_rows = pay.shape[0]
 
     barrier = pltpu.get_barrier_semaphore()
 
@@ -303,10 +392,6 @@
     for step in range(sample_peers):
         greet(left, lax.rem(mine + step, sample_peers))
         greet(right, lax.rem(mine + step, sample_peers))
-
-    @pl.loop(2, atom_peers - 1)
-    def _(step):
-        greet(lax.rem(me + step, atom_peers), mine)
 
     own_copy = pltpu.make_async_copy(single, single_ext.at[pl.ds(HALO, rows)], own_sem)
     own_copy.start()
@@ -317,17 +402,7 @@
     )
     for d in range(3):
         cx[d : d + 1, pl.ds(HALO, rows)] = (true[d : d + 1, :] + sigma[0] * noise[d]) * inv
-    blocks = rows // PAIR_BLK
-    for d in range(3):
-        for b in range(blocks):
-            wide[d * blocks + b : d * blocks + b + 1, :] = true[
-                d : d + 1, b * PAIR_BLK : (b + 1) * PAIR_BLK
-            ]
-    for b in range(blocks):
-        wide[3 * blocks + b : 3 * blocks + b + 1, :] = jnp.full((1, PAIR_BLK), counts[b], jnp.int32).astype(f32)
-    pay[...] = wide[...].astype(bf16)
-    gathered[pl.ds(pl.multiple_of(me * pay_rows, pay_rows), pay_rows), :] = pay[...]
-    pl.semaphore_wait(barrier, 7 + 2 * sample_peers + atom_peers - 3)
+    pl.semaphore_wait(barrier, 3 * sample_peers - 1)
 
     def part_copy(step):
         peer = lax.rem(mine + step, sample_peers)
@@ -392,17 +467,6 @@
             for step in range(sample_peers):
                 edge_copy(i, step).start()
 
-    def all_copy(step):
-        at = pl.ds(pl.multiple_of(me * pay_rows, pay_rows), pay_rows)
-        return remote(
-            pay, gathered.at[at], all_send.at[step], all_recv.at[step],
-            lax.rem(me + step, atom_peers), mine,
-        )
-
-    @pl.loop(1, atom_peers)
-    def _(step):
-        all_copy(step).start()
-
     for copy in parts:
         copy.wait_send()
     for copy in near:
@@ -417,41 +481,7 @@
             for step in range(sample_peers):
                 edge_copy(i, step).wait_send()
 
-    @pl.loop(1, atom_peers)
-    def _(step):
-        all_copy(step).wait()
-
     own_copy.wait()
-
-
-def spread_kernel(atom_peers, pay, gathered, send, recv):
-    me = lax.axis_index("atoms")
-    mine = lax.axis_index("samples")
-    rows = pay.shape[0]
-    barrier = pltpu.get_barrier_semaphore()
-
-    @pl.loop(1, atom_peers)
-    def _(step):
-        pl.semaphore_signal(
-            barrier, inc=1, device_id=(lax.rem(me + step, atom_peers), mine), device_id_type=MESH
-        )
-
-    at = pl.ds(pl.multiple_of(me * rows, rows), rows)
-    gathered[at, :] = pay[...]
-    pl.semaphore_wait(barrier, atom_peers - 1)
-
-    def copy(step):
-        return remote(
-            pay, gathered.at[at], send.at[step], recv.at[step], lax.rem(me + step, atom_peers), mine
-        )
-
-    @pl.loop(1, atom_peers)
-    def _(step):
-        copy(step).start()
-
-    @pl.loop(1, atom_peers)
-    def _(step):
-        copy(step).wait()
 
 
 def vmem(n):
@@ -462,27 +492,38 @@
     return [pl.BlockSpec(memory_space=pltpu.SMEM)] * n
 
 
-def run_atoms(place, sigma, single, cx, tok, coord_in, w_qkv, w_o, w_gu, w_down, gains, w_out):
+def run_atoms(sigma, counts, true, single, cx, tok, coord_in, w_qkv, w_o, w_gu, w_down, gains, w_out):
     ext = single.shape[0]
     rows = ext - 2 * HALO
+    blocks = rows // PAIR_BLK
+    atom_peers = lax.axis_size("atoms")
+    dma = pltpu.SemaphoreType.DMA
+    one_gather = [dma((DEPTH,)), dma((DEPTH,)), dma((atom_peers,)), dma((atom_peers,))]
     return pl.pallas_call(
-        atoms_kernel,
+        functools.partial(atoms_kernel, atom_peers),
         name="atoms",
         out_shape=(
             jax.ShapeDtypeStruct((8, rows), f32),
-            jax.ShapeDtypeStruct((3 * (rows // PAIR_BLK), PAIR_BLK), bf16),
+            jax.ShapeDtypeStruct((atom_peers * 3 * blocks, PAIR_BLK), bf16),
+            jax.ShapeDtypeStruct((atom_peers * 4 * blocks, PAIR_BLK), bf16),
         ),
-        in_specs=smem(2) + vmem(10),
-        out_specs=tuple(vmem(2)),
+        in_specs=smem(2) + vmem(11),
+        out_specs=tuple(vmem(3)),
         scratch_shapes=[
             pltpu.VMEM((ext, CHANNELS), f32),
             pltpu.VMEM((2, ext, 2 * CHANNELS), bf16),
             pltpu.VMEM((2, ext // QBLK, CHANNELS, CHANNELS), bf16),
             pltpu.VMEM((ext, CHANNELS), f32),
-            pltpu.VMEM((3 * (rows // PAIR_BLK), PAIR_BLK), f32),
-        ],
-        compiler_params=pltpu.CompilerParams(vmem_limit_bytes=VMEM_LIMIT),
-    )(place, sigma, single, cx, tok, coord_in, w_qkv, w_o, w_gu, w_down, gains, w_out.T)
+            pltpu.VMEM((3 * blocks, PAIR_BLK), bf16),
+            pltpu.VMEM((4 * blocks, PAIR_BLK), bf16),
+            pltpu.VMEM((4 * blocks, PAIR_BLK), f32),
+        ]
+        + one_gather
+        + one_gather,
+        compiler_params=pltpu.CompilerParams(
+            collective_id=1, has_side_effects=True, vmem_limit_bytes=VMEM_LIMIT
+        ),
+    )(sigma, counts, true, single, cx, tok, coord_in, w_qkv, w_o, w_gu, w_down, gains, w_out.T)
 
 
 def run_pairs(sigma, counts, partners, gathered_pred, gathered_true, pred, true):
@@ -505,10 +546,9 @@
     return jnp.swapaxes(coord_grad, 0, 1), jnp.swapaxes(lddt_grad, 0, 1)
 
 
-def share(sigma, feats, proj, single, token, true, noise, counts):
+def share(sigma, feats, proj, single, token, true, noise):
     atom_peers, sample_peers = lax.axis_size("atoms"), lax.axis_size("samples")
     rows, tokens = single.shape[0], feats.shape[1]
-    blocks = rows // PAIR_BLK
     part = tokens // sample_peers
     dma = pltpu.SemaphoreType.DMA
     return pl.pallas_call(
@@ -518,59 +558,35 @@
             jax.ShapeDtypeStruct((tokens + 2 * TOK_HALO, CHANNELS), bf16),
             jax.ShapeDtypeStruct((rows + 2 * HALO, CHANNELS), bf16),
             jax.ShapeDtypeStruct((8, rows + 2 * HALO), f32),
-            jax.ShapeDtypeStruct((atom_peers * 4 * blocks, PAIR_BLK), bf16),
         ),
-        in_specs=smem(2) + vmem(6),
-        out_specs=tuple(vmem(4)),
+        in_specs=smem(1) + vmem(6),
+        out_specs=tuple(vmem(3)),
         scratch_shapes=[
             pltpu.VMEM((tokens, CHANNELS), f32),
             pltpu.VMEM((sample_peers, part, CHANNELS), f32),
             pltpu.VMEM((part, CHANNELS), bf16),
-            pltpu.VMEM((4 * blocks, PAIR_BLK), bf16),
-            pltpu.VMEM((4 * blocks, PAIR_BLK), f32),
             dma((sample_peers,)), dma((sample_peers,)), dma((sample_peers,)), dma((sample_peers,)),
             dma((sample_peers,)), dma((4,)), dma((4,)), dma((4,)),
-            dma((atom_peers,)), dma((atom_peers,)), dma,
+            dma,
         ],
         compiler_params=pltpu.CompilerParams(
             collective_id=0, has_side_effects=True, vmem_limit_bytes=VMEM_LIMIT
         ),
-    )(sigma, counts, feats, proj, single, token, true, noise)
-
-
-def spread(pay):
-    atom_peers = lax.axis_size("atoms")
-    dma = pltpu.SemaphoreType.DMA
-    return pl.pallas_call(
-        functools.partial(spread_kernel, atom_peers),
-        name="spread",
-        out_shape=jax.ShapeDtypeStruct((atom_peers * pay.shape[0], pay.shape[1]), pay.dtype),
-        in_specs=vmem(1),
-        out_specs=vmem(1)[0],
-        scratch_shapes=[dma((atom_peers,)), dma((atom_peers,))],
-        compiler_params=pltpu.CompilerParams(
-            collective_id=1, has_side_effects=True, vmem_limit_bytes=VMEM_LIMIT
-        ),
-    )(pay)
+    )(sigma, feats, proj, single, token, true, noise)
 
 
 def on_device(
     token_feats, proj_w, atom_single, atom_token, true_coords, noise, sigma, coord_in,
     w_qkv, w_o, w_gu, w_down, gains, w_out, pair_blocks, pair_count,
 ):
-    rank = lax.axis_index("atoms")
-    rows = atom_single.shape[0]
-    tok, single, cx, gathered_true = share(
+    tok, single, cx = share(
         sigma, token_feats.T, proj_w, atom_single, atom_token[None], true_coords,
-        jnp.swapaxes(noise, 0, 1), pair_count,
-    )
-    place = jnp.stack(
-        [rank * rows, jnp.int32(rows * lax.axis_size("atoms")), rank * token_feats.shape[0]]
-    ).astype(jnp.int32)
-    pred, pay = run_atoms(
-        place, sigma, single, cx, tok, coord_in, w_qkv, w_o, w_gu, w_down, gains, w_out
-    )
-    gathered_pred = spread(pay)
+        jnp.swapaxes(noise, 0, 1),
+    )
+    pred, gathered_pred, gathered_true = run_atoms(
+        sigma, pair_count, true_coords, single, cx, tok,
+        coord_in, w_qkv, w_o, w_gu, w_down, gains, w_out,
+    )
     return run_pairs(
         sigma, pair_count, pair_blocks, gathered_pred, gathered_true, pred, true_coords
     )

time: 95.4 us -> 80 us (0.84)
  the two profiles are of different devices: /device:TPU:166 before, /device:TPU:6 now
where the time goes in v3:
time: 80 us; the launch traced here: 79.1 us
  Pallas kernels  77.8 us (97%)
  between operations  1.29 us (2%)
    pallas_call x1, Pallas kernels, run_atoms(): pl.pallas_call(functools.partial(atoms_kernel, atom_peers), name='atoms',...  37.8 us
    pallas_call x1, Pallas kernels, run_pairs(): pl.pallas_call(pairs_kernel, name='pairs', out_shape=(out, out), in_specs...  20.7 us
    pallas_call x1, Pallas kernels, share(): pl.pallas_call(functools.partial(share_kernel, atom_peers, sample_peers),...  19.4 us

profile of v3, /device:TPU:6, one launch (start us, length us, event | category | flops | bytes accessed | tf_op | source)
XLA Modules:
  0.0 79.1 jit_solution(403119052546080636)
XLA Ops:
  1.3 19.4 %share.1 = (bf16[352,128]{1,0:T(8,128)(2,1)}, bf16[2560,128]{1,0:T(8,128)(2,1)}, f32[8,2560]{1,0:T(8,128)}) custom-call(f32[1]{0:T(128)S(6)} %copy.18.sigma, bf16[96,256]{1,0:T(8,128)(2,1)} %bitcast.6, bf16[96,128]{1,0:T(8,128)(2,1)} %proj.1, bf16[2048,128]{1,0:T(8,128)(2,1)} %single.1, s32[1,2048]{1,0:T(1,128)} %bitcast.8, f32[3,2048]{1,0:T(4,128)} %true.5, ...), custom_call_target="tpu_custom_call" | custom-call | tf_op jit(solution)/shard_map/share/pallas_call | solution.py:554
  20.7 37.8 %atoms.1 = (f32[8,2048]{1,0:T(8,128)}, bf16[1536,128]{1,0:T(8,128)(2,1)}, bf16[2048,128]{1,0:T(8,128)(2,1)}) custom-call(f32[1]{0:T(128)S(6)} %copy.18.sigma, s32[16]{0:T(128)} %counts.3, f32[3,2048]{1,0:T(4,128)} %true.5, bf16[2560,128]{1,0:T(8,128)(2,1)} %get-tuple-element.10.single, f32[8,2560]{1,0:T(8,128)} %get-tuple-element.11.cx, ...), custom_call_target="tpu_custom_call" | custom-call | tf_op jit(solution)/shard_map/atoms/pallas_call | solution.py:502
  58.5 20.7 %pairs.1 = (f32[3,1,2048]{2,1,0:T(1,128)}, f32[3,1,2048]{2,1,0:T(1,128)}) custom-call(f32[1]{0:T(128)S(6)} %copy.18.sigma, s32[16]{0:T(128)} %counts.3, s32[16,13]{1,0:T(8,128)} %partners.1, bf16[1536,128]{1,0:T(8,128)(2,1)} %get-tuple-element.13.gathered_pred, bf16[2048,128]{1,0:T(8,128)(2,1)} %get-tuple-element.14.gathered_true, ...), custom_call_target="tpu_custom_call" | custom-call | tf_op jit(solution)/shard_map/pairs/pallas_call | solution.py:533

commit v4 on v3

v4 whole, which is shorter than its diff:
```python
import functools
import math

import jax
import jax.numpy as jnp
from jax import lax
from jax.experimental import pallas as pl
from jax.experimental.pallas import tpu as pltpu
from jax.sharding import PartitionSpec as P

HEADS = 4
HEAD_DIM = 32
FF_ATOM = 256
LAYERS = 3
QBLK = 32
KWIN = 128
PAIR_BLK = 128
CHANNELS = 128
CHUNK = 256
FIRST_UNROLL = 5
UNROLL = 4
HALO = 256
TOK_HALO = 48
TOK_WIN = 64
EPS = 1e-05
DEPTH = 8
VMEM_LIMIT = 56 * 1024 * 1024

f32 = jnp.float32
bf16 = jnp.bfloat16


def dot(a, b, dims=((1,), (0,)), precision=None):
    return lax.dot_general(a, b, (dims, ((), ())), precision=precision, preferred_element_type=f32)


def pieces(v):
    hi = v.astype(bf16).astype(f32)
    mid = (v - hi).astype(bf16).astype(f32)
    lo = (v - hi - mid).astype(bf16).astype(f32)
    return hi, mid, lo


def rms_scale(h):
    return h * lax.rsqrt(jnp.mean(h * h, axis=1, keepdims=True) + EPS)


MESH = pl.DeviceIdType.MESH


def remote(src, dst, send, recv, atom, sample):
    return pltpu.make_async_remote_copy(
        src_ref=src, dst_ref=dst, send_sem=send, recv_sem=recv,
        device_id=(atom, sample), device_id_type=MESH,
    )

def gather_plan(atom_peers):
    nz = DEPTH
    nx = atom_peers // nz
    me = lax.axis_index("atoms")
    x, z = me // nz, lax.rem(me, nz)

    def along_z(dz):
        return x * nz + lax.rem(z + dz + nz, nz)

    def along_x(dx):
        return lax.rem(x + dx, nx) * nz + z

    return nz, nx, me, along_z, along_x


class Gather:
    def __init__(self, atom_peers, pay, whole, sems):
        self.nz, self.nx, self.me, self.along_z, self.along_x = gather_plan(atom_peers)
        self.mine = lax.axis_index("samples")
        self.pay, self.whole = pay, whole
        self.z_send, self.z_recv, self.x_send, self.x_recv = sems
        self.order = [0]
        for step in range(1, self.nz // 2 + 1):
            self.order += [step, self.nz - step] if 2 * step != self.nz else [step]

    def rows(self, owner):
        size = self.pay.shape[0]
        return pl.ds(pl.multiple_of(owner * size, size), size)

    def z_copy(self, dz):
        return remote(
            self.pay, self.whole.at[self.rows(self.me)], self.z_send.at[dz], self.z_recv.at[dz],
            self.along_z(dz), self.mine,
        )

    def x_copy(self, dz, dx):
        at = self.rows(self.along_z(-dz))
        src = self.pay if dz == 0 else self.whole.at[at]
        slot = dz * self.nx + dx
        return remote(
            src, self.whole.at[at], self.x_send.at[slot], self.x_recv.at[slot],
            self.along_x(dx), self.mine,
        )

    def start(self):
        for dz in self.order[1:]:
            self.z_copy(dz).start()
        for dx in range(1, self.nx):
            self.x_copy(0, dx).start()
        self.whole[self.rows(self.me), :] = self.pay[...]

    def forward(self):
        for dz in self.order[1:]:
            self.z_copy(dz).wait_recv()
            for dx in range(1, self.nx):
                self.x_copy(dz, dx).start()

    def finish(self):
        for dz in self.order[1:]:
            self.z_copy(dz).wait_send()
        for dz in self.order:
            for dx in range(1, self.nx):
                self.x_copy(dz, dx).wait()


def atoms_kernel(
    atom_peers, sample_peers, sigma, counts, feats, proj, own_single, token, true, noise,
    coord_in, wqkv, wo, wgu, wdown, gains, wout,
    pred, gathered_pred, gathered_true,
    hid, kv, queries, bias, pay, true_pay, wide, tok, single, cx, partial, arrived, slab, *sems,
):
    rows = own_single.shape[0]
    ext = single.shape[0]
    blocks = rows // PAIR_BLK
    half = blocks // 2
    nz, nx, me, along_z, along_x = gather_plan(atom_peers)
    mine = lax.axis_index("samples")
    barrier = pltpu.get_barrier_semaphore()
    right = lax.rem(me + 1, atom_peers)
    left = lax.rem(me + atom_peers - 1, atom_peers)
    share = feats.shape[1] // sample_peers
    (part_send, part_recv, tok_send, tok_recv, edge_send, edge_recv, near_send, near_recv,
     own_sem) = sems[:9]

    def greet(atom, sample):
        pl.semaphore_signal(barrier, inc=1, device_id=(atom, sample), device_id_type=MESH)

    for step in range(1, sample_peers):
        greet(me, lax.rem(mine + step, sample_peers))
    for step in range(sample_peers):
        greet(left, lax.rem(mine + step, sample_peers))
        greet(right, lax.rem(mine + step, sample_peers))

    for dz in range(1, nz):
        greet(along_z(dz), mine)
    for dx in range(1, nx):
        greet(along_x(dx), mine)
    first_atom = me * rows
    total_atoms = rows * atom_peers
    first_tok = me * (tok.shape[0] - 2 * TOK_HALO)
    sig = sigma[0]
    inv = lax.rsqrt(jnp.full((8, CHANNELS), sig * sig + 4.0, f32))[0:1, 0:1]
    zero5 = jnp.zeros((5, CHANNELS), f32)
    hi, mid, lo = pieces(jnp.concatenate([coord_in[...], zero5], axis=0))
    coord_w = jnp.concatenate([hi, mid, lo, hi, mid, hi], axis=0).astype(bf16)
    head = jnp.concatenate([wout[...], jnp.zeros((CHANNELS - 3, CHANNELS), f32)], axis=0).T
    hi, mid, lo = pieces(head)
    head = jnp.concatenate([hi, hi, mid], axis=0).astype(bf16)
    q_scale = math.log2(math.e) / math.sqrt(HEAD_DIM)
    lane = lax.broadcasted_iota(jnp.int32, (1, CHANNELS), 1) // HEAD_DIM

    pos = first_atom - HALO + lax.broadcasted_iota(jnp.int32, (ext, CHANNELS), 0)
    own_copy = pltpu.make_async_copy(own_single, single.at[pl.ds(HALO, rows)], own_sem)
    own_copy.start()
    partial[...] = dot(feats[...], proj[...], ((0,), (0,)))
    cx[3:8, pl.ds(HALO, rows)] = jnp.concatenate(
        [token[...].astype(f32), jnp.zeros((4, rows), f32)], axis=0
    )
    for d in range(3):
        cx[d : d + 1, pl.ds(HALO, rows)] = (true[d : d + 1, :] + sig * noise[d]) * inv
    for d in range(3):
        for b in range(blocks):
            wide[d * blocks + b : d * blocks + b + 1, :] = true[
                d : d + 1, b * PAIR_BLK : (b + 1) * PAIR_BLK
            ]
    for b in range(blocks):
        wide[3 * blocks + b : 3 * blocks + b + 1, :] = jnp.full((1, PAIR_BLK), counts[b], jnp.int32).astype(f32)
    true_pay[...] = wide[...].astype(bf16)
    bias[...] = jnp.where((pos >= 0) & (pos < total_atoms), 0.0, -1e30)
    pl.semaphore_wait(barrier, 3 * sample_peers - 1 + nz + nx - 2)
    true_gather = Gather(atom_peers, true_pay, gathered_true, sems[9:13])
    pred_gathers = [
        Gather(
            atom_peers, pay.at[i], gathered_pred.at[pl.ds(i * (atom_peers * 4 * half), atom_peers * 4 * half)],
            sems[13 + 4 * i : 17 + 4 * i],
        )
        for i in range(2)
    ]

    def part_copy(step):
        peer = lax.rem(mine + step, sample_peers)
        at = pl.multiple_of(peer * share, share)
        return remote(
            partial.at[pl.ds(at, share)], arrived.at[step], part_send.at[step], part_recv.at[step],
            me, peer,
        )

    parts = [part_copy(step) for step in range(1, sample_peers)]
    for copy in parts:
        copy.start()
    near = [
        remote(own_single.at[pl.ds(rows - HALO, HALO)], single.at[pl.ds(0, HALO)],
               near_send.at[0], near_recv.at[0], right, mine),
        remote(own_single.at[pl.ds(0, HALO)], single.at[pl.ds(rows + HALO, HALO)],
               near_send.at[1], near_recv.at[1], left, mine),
        remote(cx.at[:, pl.ds(rows, HALO)], cx.at[:, pl.ds(0, HALO)],
               near_send.at[2], near_recv.at[2], right, mine),
        remote(cx.at[:, pl.ds(HALO, HALO)], cx.at[:, pl.ds(rows + HALO, HALO)],
               near_send.at[3], near_recv.at[3], left, mine),
    ]
    for copy in near:
        copy.start()
    for copy in parts:
        copy.wait_recv()
    total = partial[pl.ds(pl.multiple_of(mine * share, share), share), :]
    for step in range(1, sample_peers):
        total = total + arrived[step]
    slab[...] = total.astype(bf16)
    my_rows = pl.ds(pl.multiple_of(TOK_HALO + mine * share, 16), share)
    tok[my_rows, :] = slab[...]

    def tok_copy(step):
        return remote(
            slab, tok.at[my_rows], tok_send.at[step], tok_recv.at[step],
            me, lax.rem(mine + step, sample_peers),
        )

    toks = [tok_copy(step) for step in range(1, sample_peers)]
    for copy in toks:
        copy.start()
    tokens = tok.shape[0] - 2 * TOK_HALO
    rest = TOK_HALO - share
    edges = (
        (sample_peers - 1, pl.ds(0, share), pl.ds(rest, share), right),
        (sample_peers - 2, pl.ds(share - rest, rest), pl.ds(0, rest), right),
        (0, pl.ds(0, share), pl.ds(TOK_HALO + tokens, share), left),
        (1, pl.ds(0, rest), pl.ds(TOK_HALO + tokens + share, rest), left),
    )

    def edge_copy(i, step):
        _, src, dst, to = edges[i]
        return remote(
            slab.at[src], tok.at[dst], edge_send.at[step], edge_recv.at[i],
            to, lax.rem(mine + step, sample_peers),
        )

    for i, edge in enumerate(edges):
        @pl.when(mine == edge[0])
        def _(i=i):
            for step in range(sample_peers):
                edge_copy(i, step).start()

    for copy in parts:
        copy.wait_send()
    for copy in near:
        copy.wait()
    for copy in toks:
        copy.wait()
    for i, edge in enumerate(edges):
        edge_copy(i, 0).wait_recv()

        @pl.when(mine == edge[0])
        def _(i=i):
            for step in range(sample_peers):
                edge_copy(i, step).wait_send()

    own_copy.wait()
    true_gather.start()

    def project(layer, at, h):
        normed = (rms_scale(h) * gains[layer, 0:1, :]).astype(bf16)
        out = dot(normed, wqkv[layer])
        rows_at = pl.ds(at, h.shape[0])
        kv[layer % 2, rows_at, :] = out[:, 128:].astype(bf16)
        for t in range(h.shape[0] // CHANNELS):
            turned = (out[t * CHANNELS : (t + 1) * CHANNELS, :128] * q_scale).T
            shifted = [turned if r == 0 else pltpu.roll(turned, r * QBLK, 1) for r in range(HEADS)]
            for w in range(CHANNELS // QBLK):
                spread = jnp.concatenate(
                    [
                        jnp.where(lane == h, shifted[(h - w) % HEADS][h * QBLK : (h + 1) * QBLK], 0.0)
                        for h in range(HEADS)
                    ],
                    axis=0,
                )
                queries[layer % 2, at // QBLK + t * HEADS + w] = spread.astype(bf16)

    def first(k, _):
        at = pl.multiple_of(k * CHUNK, CHUNK)
        c = cx[:, pl.ds(at, CHUNK)]
        hi, mid, lo = pieces(c)
        rel = c[3:4, :].astype(jnp.int32) - (first_tok - TOK_HALO + k * (CHUNK // 8))
        hot = jnp.where(lax.broadcasted_iota(jnp.int32, (TOK_WIN, CHUNK), 0) == rel, 1.0, 0.0)
        left = jnp.concatenate([hot, hi, hi, hi, mid, mid, lo], axis=0).astype(bf16)
        tok_at = pl.ds(pl.multiple_of(k * (CHUNK // 8), CHUNK // 8), TOK_WIN)
        right = jnp.concatenate([tok[tok_at, :], coord_w], axis=0)
        h = single[pl.ds(at, CHUNK), :].astype(f32) + dot(left, right, ((0,), (0,)))
        hid[pl.ds(at, CHUNK), :] = h
        project(0, at, h)
        return 0

    lax.fori_loop(0, ext // CHUNK, first, 0, unroll=FIRST_UNROLL)

    true_gather.forward()

    def attend(layer, at, size):
        buf = layer % 2
        outs = []
        for w in range(size // QBLK):
            keys_at = pl.ds(at + (w * QBLK - 48), KWIN)
            keys = kv[buf, keys_at, 0:128]
            values = kv[buf, keys_at, 128:256]
            scores = dot(keys, queries[buf, at // QBLK + w]) + bias[keys_at, :]
            top = jnp.max(scores, axis=0, keepdims=True)
            weights = jnp.exp2(scores - top)
            weights = (weights * (1.0 / jnp.sum(weights, axis=0, keepdims=True))).astype(bf16)
            both = dot(weights, values, ((0,), (0,)))
            out = both[0:QBLK]
            for h in range(1, HEADS):
                out = jnp.where(lane == h, both[h * QBLK : (h + 1) * QBLK], out)
            outs.append(out.astype(bf16))
        return jnp.concatenate(outs, axis=0)

    def block(layer, at, size):
        h = hid[pl.ds(at, size), :]
        h = h + dot(attend(layer, at, size), wo[layer])
        normed = (rms_scale(h) * gains[layer, 1:2, :]).astype(bf16)
        gu = dot(normed, wgu[layer])
        gate = 0.5 * gu[:, :FF_ATOM]
        inner = (gate * (1.0 + jnp.tanh(gate)) * gu[:, FF_ATOM:]).astype(bf16)
        h = h + dot(inner, wdown[layer])
        if layer + 1 < LAYERS:
            hid[pl.ds(at, size), :] = h
            project(layer + 1, at, h)
        else:
            normed = rms_scale(h)
            hi = normed.astype(bf16)
            mid = (normed - hi.astype(f32)).astype(bf16)
            update = dot(jnp.concatenate([hi, mid, hi], axis=1), head)
            update = jnp.concatenate(
                [update[t * CHANNELS : (t + 1) * CHANNELS].T[0:8] for t in range(size // CHANNELS)],
                axis=1,
            )
            noisy = cx[:, pl.ds(at, size)]
            out = inv * (4.0 * noisy + (2.0 * sig) * update)
            pred[:, pl.ds(pl.multiple_of(at - HALO, 128), size)] = out
            part = (at - HALO) // (half * PAIR_BLK)
            for d in range(3):
                for i in range(half):
                    wide[d * half + i : d * half + i + 1, :] = out[
                        d : d + 1, i * PAIR_BLK : (i + 1) * PAIR_BLK
                    ]
            pay[part] = wide[0 : 4 * half, :].astype(bf16)

    middle = HALO + rows // 2
    start = HALO - 128
    end = HALO + rows + 128
    block(0, start, middle + 256 - start)
    block(1, start, middle + 128 - start)
    block(2, HALO, rows // 2)
    pred_gathers[0].start()
    block(0, middle + 256, end - middle - 256)
    pred_gathers[0].forward()
    block(1, middle + 128, end - middle - 128)
    block(2, middle, rows // 2)
    pred_gathers[1].start()
    pred_gathers[1].forward()
    true_gather.finish()
    pred_gathers[0].finish()
    pred_gathers[1].finish()


def pairs_kernel(
    sigma, counts, partners, gathered_pred, gathered_true, pred, true,
    coord_grad, lddt_grad, wide_pred, wide_true, owns, totals, held, parts,
):
    blocks = counts.shape[0]
    wide_pred[...] = gathered_pred[...].astype(f32)
    wide_true[...] = gathered_true[...].astype(f32)
    peers = gathered_true.shape[0] // (4 * blocks)
    listed = jnp.zeros((blocks, PAIR_BLK), f32)
    for peer in range(peers):
        listed = listed + wide_true[peer * 4 * blocks + 3 * blocks : (peer + 1) * 4 * blocks, :]
    listed = jnp.sum(listed, axis=0, keepdims=True)
    total_pairs = listed * (PAIR_BLK * PAIR_BLK) - float(PAIR_BLK * blocks * peers)
    pair_scale = -0.0625 * (blocks * peers * PAIR_BLK * PAIR_BLK) / total_pairs
    row8 = lax.broadcasted_iota(jnp.int32, (8, PAIR_BLK), 0)
    row4 = row8 & 3
    diff = lax.broadcasted_iota(jnp.int32, (PAIR_BLK, PAIR_BLK), 0) - lax.broadcasted_iota(
        jnp.int32, (PAIR_BLK, PAIR_BLK), 1
    )

    half = blocks // 2

    def partner_rows(wide, base, stride):
        x, y, z = (wide[pl.ds(base + d * stride, 1), :] for d in range(3))
        n1, n2, n3 = pieces(x * x + y * y + z * z)
        xyz = jnp.where(row4 == 0, x, jnp.where(row4 == 1, y, z))
        upper = jnp.where(row4 == 3, jnp.where(row8 == 3, n1, n2), xyz)
        ones = jnp.where(row8 < 7, 1.0, 0.0)
        lower = jnp.where(row8 < 3, xyz, jnp.where(row8 == 3, n3, ones))
        return jnp.concatenate([upper, lower], axis=0)

    def own_rows(x, y, z):
        n = x * x + y * y + z * z + 1.0
        n1, n2, n3 = pieces(0.25 * n)
        xp, yp, zp = pieces(-0.5 * x), pieces(-0.5 * y), pieces(-0.5 * z)

        def xyz(i):
            return jnp.where(row4 == 0, xp[i], jnp.where(row4 == 1, yp[i], zp[i]))

        upper = jnp.where(row4 == 3, 0.25, jnp.where(row8 < 4, xyz(0), xyz(1)))
        norms = jnp.where(row8 == 4, n1, jnp.where(row8 == 5, n2, n3))
        norms = jnp.where(row8 == 7, 0.0, norms)
        lower = jnp.where(row8 < 3, xyz(2), jnp.where(row8 == 3, 0.25, norms))
        return jnp.concatenate([upper, lower], axis=0)

    none = jnp.zeros((16, PAIR_BLK), f32)
    square = sigma[0] * sigma[0]
    mse_scale = jnp.full((1, PAIR_BLK), square + 4.0, f32) / jnp.full((1, PAIR_BLK), 6.0 * square, f32)
    totals[...] = jnp.zeros_like(totals)
    owns[blocks] = jnp.zeros(owns.shape[1:], bf16) + 1.0
    for b in range(blocks):
        at = slice(b * PAIR_BLK, (b + 1) * PAIR_BLK)
        own_pred = own_rows(*(pred[d : d + 1, at] for d in range(3)))
        own_true = own_rows(*(true[d : d + 1, at] for d in range(3)))
        owns[b] = jnp.concatenate(
            [
                jnp.concatenate([own_pred, none], axis=1),
                jnp.concatenate([none, own_true], axis=1),
            ],
            axis=0,
        ).astype(bf16)

    def begin(b, m):
        known = jnp.minimum(b, blocks - 1)
        p = partners[known, m]
        owner, place = p // blocks, p % blocks
        at = place // half * (peers * 4 * half) + owner * (4 * half) + place % half
        part_pred = partner_rows(wide_pred, at, half)
        part_true = partner_rows(wide_true, owner * (4 * blocks) + place, blocks)
        part = jnp.concatenate([part_pred, part_true], axis=0).astype(bf16)
        squares = dot(part, owns[b], ((0,), (0,)))
        last = m + 1 >= counts[known]
        after = jnp.where(last, jnp.minimum(b + 1, blocks), b), jnp.where(last, 0, m + 1)
        return part, squares, after

    def middle(squares, m):
        sp, st = squares[:, :PAIR_BLK], squares[:, PAIR_BLK:]
        rp = lax.rsqrt(sp)
        gap = sp * rp - st * lax.rsqrt(st)
        e2 = gap * gap + 0.0025
        re = lax.rsqrt(e2)
        err = e2 * re
        th = [jnp.tanh(0.5 * t - err) for t in (0.5, 1.0, 2.0, 4.0)]
        slope = 4.0 - (th[0] * th[0] + th[1] * th[1] + th[2] * th[2] + th[3] * th[3])
        coef = slope * gap * (re * rp)
        shut = jnp.where(m == 0, 0, 2 * PAIR_BLK)
        return jnp.where(diff == shut, 0.0, coef).astype(bf16)

    def start(slot, b, m):
        begun = []
        for i in range(UNROLL):
            part, squares, after = begin(b, m)
            parts[slot, i] = part[0:16]
            held[slot, i] = squares
            begun.append((b, m))
            b, m = after
        return begun, (b, m)

    def end(slot, begun):
        coefs = [middle(held[slot, i], m) for i, (_, m) in enumerate(begun)]
        found = [(b, dot(parts[slot, i], coef)[8:16]) for i, ((b, _), coef) in enumerate(zip(begun, coefs))]
        for at, sums in found:
            totals[at] = totals[at] + sums

    def visit(_, carry):
        begun, place = carry
        more, place = start(1, *place)
        end(0, begun)
        begun, place = start(0, *place)
        end(1, more)
        return begun, place

    live = counts[0]
    for b in range(1, blocks):
        live = live + counts[b]
    lax.fori_loop(0, (live + 2 * UNROLL - 1) // (2 * UNROLL), visit, start(0, jnp.int32(0), jnp.int32(0)))

    for b in range(blocks):
        at = slice(b * PAIR_BLK, (b + 1) * PAIR_BLK)
        total = totals[b]
        for d in range(3):
            pc, tc = pred[d : d + 1, at], true[d : d + 1, at]
            lg = pair_scale[:, 0:PAIR_BLK] * (pc * total[4:5] - total[d : d + 1])
            lddt_grad[d, :, at] = lg
            coord_grad[d, :, at] = mse_scale * (pc - tc) - lg * (1.0 / PAIR_BLK)


def vmem(n):
    return [pl.BlockSpec(memory_space=pltpu.VMEM)] * n


def smem(n):
    return [pl.BlockSpec(memory_space=pltpu.SMEM)] * n


def run_atoms(
    sigma, counts, feats, proj, single, token, true, noise,
    coord_in, w_qkv, w_o, w_gu, w_down, gains, w_out,
):
    rows, tokens = single.shape[0], feats.shape[1]
    ext = rows + 2 * HALO
    blocks = rows // PAIR_BLK
    atom_peers, sample_peers = lax.axis_size("atoms"), lax.axis_size("samples")
    part = tokens // sample_peers
    dma = pltpu.SemaphoreType.DMA
    one_gather = [dma((DEPTH,)), dma((DEPTH,)), dma((atom_peers,)), dma((atom_peers,))]
    return pl.pallas_call(
        functools.partial(atoms_kernel, atom_peers, sample_peers),
        name="atoms",
        out_shape=(
            jax.ShapeDtypeStruct((8, rows), f32),
            jax.ShapeDtypeStruct((atom_peers * 4 * blocks, PAIR_BLK), bf16),
            jax.ShapeDtypeStruct((atom_peers * 4 * blocks, PAIR_BLK), bf16),
        ),
        in_specs=smem(2) + vmem(13),
        out_specs=tuple(vmem(3)),
        scratch_shapes=[
            pltpu.VMEM((ext, CHANNELS), f32),
            pltpu.VMEM((2, ext, 2 * CHANNELS), bf16),
            pltpu.VMEM((2, ext // QBLK, CHANNELS, CHANNELS), bf16),
            pltpu.VMEM((ext, CHANNELS), f32),
            pltpu.VMEM((2, 2 * blocks, PAIR_BLK), bf16),
            pltpu.VMEM((4 * blocks, PAIR_BLK), bf16),
            pltpu.VMEM((4 * blocks, PAIR_BLK), f32),
            pltpu.VMEM((tokens + 2 * TOK_HALO, CHANNELS), bf16),
            pltpu.VMEM((ext, CHANNELS), bf16),
            pltpu.VMEM((8, ext), f32),
            pltpu.VMEM((tokens, CHANNELS), f32),
            pltpu.VMEM((sample_peers, part, CHANNELS), f32),
            pltpu.VMEM((part, CHANNELS), bf16),
            dma((sample_peers,)), dma((sample_peers,)), dma((sample_peers,)), dma((sample_peers,)),
            dma((sample_peers,)), dma((4,)), dma((4,)), dma((4,)), dma,
        ]
        + 3 * one_gather,
        compiler_params=pltpu.CompilerParams(
            collective_id=0, has_side_effects=True, vmem_limit_bytes=VMEM_LIMIT
        ),
    )(
        sigma, counts, feats, proj, single, token, true, noise,
        coord_in, w_qkv, w_o, w_gu, w_down, gains, w_out.T,
    )


def run_pairs(sigma, counts, partners, gathered_pred, gathered_true, pred, true):
    rows = pred.shape[1]
    wides = [pltpu.VMEM(g.shape, f32) for g in (gathered_pred, gathered_true)]
    out = jax.ShapeDtypeStruct((3, 1, rows), f32)
    coord_grad, lddt_grad = pl.pallas_call(
        pairs_kernel,
        name="pairs",
        out_shape=(out, out),
        in_specs=smem(3) + vmem(4),
        out_specs=tuple(vmem(2)),
        scratch_shapes=wides
        + [
            pltpu.VMEM((rows // PAIR_BLK + 1, 32, 2 * PAIR_BLK), bf16),
            pltpu.VMEM((rows // PAIR_BLK + 1, 8, PAIR_BLK), f32),
            pltpu.VMEM((2, UNROLL, PAIR_BLK, 2 * PAIR_BLK), f32),
            pltpu.VMEM((2, UNROLL, 16, PAIR_BLK), bf16),
        ],
        compiler_params=pltpu.CompilerParams(vmem_limit_bytes=VMEM_LIMIT),
    )(sigma, counts, partners, gathered_pred, gathered_true, pred, true)
    return jnp.swapaxes(coord_grad, 0, 1), jnp.swapaxes(lddt_grad, 0, 1)


def on_device(
    token_feats, proj_w, atom_single, atom_token, true_coords, noise, sigma, coord_in,
    w_qkv, w_o, w_gu, w_down, gains, w_out, pair_blocks, pair_count,
):
    pred, gathered_pred, gathered_true = run_atoms(
        sigma, pair_count, token_feats.T, proj_w, atom_single, atom_token[None], true_coords,
        jnp.swapaxes(noise, 0, 1), coord_in, w_qkv, w_o, w_gu, w_down, gains, w_out,
    )
    return run_pairs(
        sigma, pair_count, pair_blocks, gathered_pred, gathered_true, pred, true_coords
    )


def solution(mesh):
    in_specs = (
        P("atoms", "samples"),
        P("samples", None),
        P("atoms", None),
        P("atoms"),
        P(None, "atoms"),
        P("samples", None, "atoms"),
        P("samples"),
        P(), P(), P(), P(), P(), P(), P(),
        P("atoms", None),
        P("atoms"),
    )
    out_specs = (P("samples", None, "atoms"), P("samples", None, "atoms"))
    return jax.shard_map(on_device, mesh=mesh, in_specs=in_specs, out_specs=out_specs, check_vma=False)
```

time: 80 us -> 70.1 us (0.88)
  Pallas kernels: 77.8 us -> 68.7 us
    pallas_call x1, Pallas kernels: 20.7 us -> 15.5 us  [run_pairs(): pl.pallas_call(pairs_kernel, name='pairs', out_shape=(out, out), in_specs...]
    pallas_call x2 -> x1, Pallas kernels: 57.2 us -> 53.1 us  [run_atoms(): pl.pallas_call(functools.partial(atoms_kernel, atom_peers, sample_peers),...]
where the time goes in v4:
time: 70.1 us; the launch traced here: 70 us
  Pallas kernels  68.7 us (98%)
  between operations  1.29 us (2%)
    pallas_call x1, Pallas kernels, run_atoms(): pl.pallas_call(functools.partial(atoms_kernel, atom_peers, sample_peers),...  53.1 us
    pallas_call x1, Pallas kernels, run_pairs(): pl.pallas_call(pairs_kernel, name='pairs', out_shape=(out, out), in_specs...  15.5 us

profile of v4, /device:TPU:6, one launch (start us, length us, event | category | flops | bytes accessed | tf_op | source)
XLA Modules:
  0.0 70.0 jit_solution(190730382212674424)
XLA Ops:
  1.3 53.1 %atoms.1 = (f32[8,2048]{1,0:T(8,128)}, bf16[2048,128]{1,0:T(8,128)(2,1)}, bf16[2048,128]{1,0:T(8,128)(2,1)}) custom-call(f32[1]{0:T(128)S(6)} %copy.18.sigma, s32[16]{0:T(128)} %counts.3, bf16[96,256]{1,0:T(8,128)(2,1)} %bitcast.6, bf16[96,128]{1,0:T(8,128)(2,1)} %proj.1, bf16[2048,128]{1,0:T(8,128)(2,1)} %own_single.1, s32[1,2048]{1,0:T(1,128)} %bitcast.8, ...), custom_call_target="tpu_custom_call" | custom-call | tf_op jit(solution)/shard_map/atoms/pallas_call | solution.py:525
  54.4 15.5 %pairs.1 = (f32[3,1,2048]{2,1,0:T(1,128)}, f32[3,1,2048]{2,1,0:T(1,128)}) custom-call(f32[1]{0:T(128)S(6)} %copy.18.sigma, s32[16]{0:T(128)} %counts.3, s32[16,13]{1,0:T(8,128)} %partners.1, bf16[2048,128]{1,0:T(8,128)(2,1)} %get-tuple-element.7.gathered_pred, bf16[2048,128]{1,0:T(8,128)(2,1)} %get-tuple-element.8.gathered_true, ...), custom_call_target="tpu_custom_call" | custom-call | tf_op jit(solution)/shard_map/pairs/pallas_call | solution.py:566

commit v5 on v4

--- a/solution.py
+++ b/solution.py
@@ -18,7 +18,7 @@
 CHANNELS = 128
 CHUNK = 256
 FIRST_UNROLL = 5
-UNROLL = 4
+UNROLL = 8
 HALO = 256
 TOK_HALO = 48
 TOK_WIN = 64
@@ -119,24 +119,61 @@
                 self.x_copy(dz, dx).wait()
 
 
+def partner_features(x, y, z):
+    row8 = lax.broadcasted_iota(jnp.int32, (8, PAIR_BLK), 0)
+    row4 = row8 & 3
+    n1, n2, n3 = pieces(x * x + y * y + z * z)
+    xyz = jnp.where(row4 == 0, x, jnp.where(row4 == 1, y, z))
+    upper = jnp.where(row4 == 3, jnp.where(row8 == 3, n1, n2), xyz)
+    ones = jnp.where(row8 < 7, 1.0, 0.0)
+    lower = jnp.where(row8 < 3, xyz, jnp.where(row8 == 3, n3, ones))
+    return jnp.concatenate([upper, lower], axis=0)
+
+
+def own_features(x, y, z):
+    row8 = lax.broadcasted_iota(jnp.int32, (8, PAIR_BLK), 0)
+    row4 = row8 & 3
+    n1, n2, n3 = pieces(0.25 * (x * x + y * y + z * z + 1.0))
+    xp, yp, zp = pieces(-0.5 * x), pieces(-0.5 * y), pieces(-0.5 * z)
+
+    def xyz(i):
+        return jnp.where(row4 == 0, xp[i], jnp.where(row4 == 1, yp[i], zp[i]))
+
+    upper = jnp.where(row4 == 3, 0.25, jnp.where(row8 < 4, xyz(0), xyz(1)))
+    norms = jnp.where(row8 == 4, n1, jnp.where(row8 == 5, n2, n3))
+    norms = jnp.where(row8 == 7, 0.0, norms)
+    lower = jnp.where(row8 < 3, xyz(2), jnp.where(row8 == 3, 0.25, norms))
+    return jnp.concatenate([upper, lower], axis=0)
+
+
+def pair_coef(squares):
+    sp, st = squares[:, :PAIR_BLK], squares[:, PAIR_BLK:]
+    rp = lax.rsqrt(sp)
+    gap = sp * rp - st * lax.rsqrt(st)
+    e2 = gap * gap + 0.0025
+    re = lax.rsqrt(e2)
+    err = e2 * re
+    th = [jnp.tanh(0.5 * t - err) for t in (0.5, 1.0, 2.0, 4.0)]
+    slope = 4.0 - (th[0] * th[0] + th[1] * th[1] + th[2] * th[2] + th[3] * th[3])
+    return slope * gap * (re * rp)
+
+
 def atoms_kernel(
     atom_peers, sample_peers, sigma, counts, feats, proj, own_single, token, true, noise,
     coord_in, wqkv, wo, wgu, wdown, gains, wout,
-    pred, gathered_pred, gathered_true,
-    hid, kv, queries, bias, pay, true_pay, wide, tok, single, cx, partial, arrived, slab, *sems,
+    pred, gathered_pred, gathered_true, owns, selves,
+    hid, kv, queries, bias, pay, true_pay, wide, tok, near_single, cx, hots, partial, arrived, slab, *sems,
 ):
     rows = own_single.shape[0]
-    ext = single.shape[0]
+    ext = rows + 2 * HALO
     blocks = rows // PAIR_BLK
-    half = blocks // 2
     nz, nx, me, along_z, along_x = gather_plan(atom_peers)
     mine = lax.axis_index("samples")
     barrier = pltpu.get_barrier_semaphore()
     right = lax.rem(me + 1, atom_peers)
     left = lax.rem(me + atom_peers - 1, atom_peers)
     share = feats.shape[1] // sample_peers
-    (part_send, part_recv, tok_send, tok_recv, edge_send, edge_recv, near_send, near_recv,
-     own_sem) = sems[:9]
+    (part_send, part_recv, tok_send, tok_recv, edge_send, edge_recv, near_send, near_recv) = sems[:8]
 
     def greet(atom, sample):
         pl.semaphore_signal(barrier, inc=1, device_id=(atom, sample), device_id_type=MESH)
@@ -166,8 +203,6 @@
     lane = lax.broadcasted_iota(jnp.int32, (1, CHANNELS), 1) // HEAD_DIM
 
     pos = first_atom - HALO + lax.broadcasted_iota(jnp.int32, (ext, CHANNELS), 0)
-    own_copy = pltpu.make_async_copy(own_single, single.at[pl.ds(HALO, rows)], own_sem)
-    own_copy.start()
     partial[...] = dot(feats[...], proj[...], ((0,), (0,)))
     cx[3:8, pl.ds(HALO, rows)] = jnp.concatenate(
         [token[...].astype(f32), jnp.zeros((4, rows), f32)], axis=0
@@ -184,14 +219,8 @@
     true_pay[...] = wide[...].astype(bf16)
     bias[...] = jnp.where((pos >= 0) & (pos < total_atoms), 0.0, -1e30)
     pl.semaphore_wait(barrier, 3 * sample_peers - 1 + nz + nx - 2)
-    true_gather = Gather(atom_peers, true_pay, gathered_true, sems[9:13])
-    pred_gathers = [
-        Gather(
-            atom_peers, pay.at[i], gathered_pred.at[pl.ds(i * (atom_peers * 4 * half), atom_peers * 4 * half)],
-            sems[13 + 4 * i : 17 + 4 * i],
-        )
-        for i in range(2)
-    ]
+    true_gather = Gather(atom_peers, true_pay, gathered_true, sems[8:12])
+    pred_gather = Gather(atom_peers, pay, gathered_pred, sems[12:16])
 
     def part_copy(step):
         peer = lax.rem(mine + step, sample_peers)
@@ -205,9 +234,9 @@
     for copy in parts:
         copy.start()
     near = [
-        remote(own_single.at[pl.ds(rows - HALO, HALO)], single.at[pl.ds(0, HALO)],
+        remote(own_single.at[pl.ds(rows - HALO, HALO)], near_single.at[0],
                near_send.at[0], near_recv.at[0], right, mine),
-        remote(own_single.at[pl.ds(0, HALO)], single.at[pl.ds(rows + HALO, HALO)],
+        remote(own_single.at[pl.ds(0, HALO)], near_single.at[1],
                near_send.at[1], near_recv.at[1], left, mine),
         remote(cx.at[:, pl.ds(rows, HALO)], cx.at[:, pl.ds(0, HALO)],
                near_send.at[2], near_recv.at[2], right, mine),
@@ -216,6 +245,22 @@
     ]
     for copy in near:
         copy.start()
+
+    def prepare(k, alone):
+        at = pl.multiple_of(k * CHUNK, CHUNK)
+        c = cx[:, pl.ds(at, CHUNK)]
+        hi, mid, lo = pieces(c)
+        coords = jnp.concatenate([hi, hi, hi, mid, mid, lo], axis=0).astype(bf16)
+        hid[pl.ds(at, CHUNK), :] = alone.astype(f32) + dot(coords, coord_w, ((0,), (0,)))
+        rel = c[3:4, :].astype(jnp.int32) - (first_tok - TOK_HALO + k * (CHUNK // 8))
+        hot = jnp.where(lax.broadcasted_iota(jnp.int32, (CHANNELS, CHUNK), 0) == rel, 1.0, 0.0)
+        hots[pl.ds(at, CHUNK), :] = hot.T.astype(bf16)
+
+    def prepare_own(k, _):
+        prepare(k, own_single[pl.ds(pl.multiple_of((k - 1) * CHUNK, CHUNK), CHUNK), :])
+        return 0
+
+    lax.fori_loop(1, 1 + rows // CHUNK, prepare_own, 0, unroll=4)
     for copy in parts:
         copy.wait_recv()
     total = partial[pl.ds(pl.multiple_of(mine * share, share), share), :]
@@ -256,21 +301,14 @@
             for step in range(sample_peers):
                 edge_copy(i, step).start()
 
-    for copy in parts:
-        copy.wait_send()
     for copy in near:
-        copy.wait()
+        copy.wait_recv()
+    prepare(0, near_single[0])
+    prepare(ext // CHUNK - 1, near_single[1])
     for copy in toks:
-        copy.wait()
-    for i, edge in enumerate(edges):
+        copy.wait_recv()
+    for i in range(len(edges)):
         edge_copy(i, 0).wait_recv()
-
-        @pl.when(mine == edge[0])
-        def _(i=i):
-            for step in range(sample_peers):
-                edge_copy(i, step).wait_send()
-
-    own_copy.wait()
     true_gather.start()
 
     def project(layer, at, h):
@@ -293,14 +331,8 @@
 
     def first(k, _):
         at = pl.multiple_of(k * CHUNK, CHUNK)
-        c = cx[:, pl.ds(at, CHUNK)]
-        hi, mid, lo = pieces(c)
-        rel = c[3:4, :].astype(jnp.int32) - (first_tok - TOK_HALO + k * (CHUNK // 8))
-        hot = jnp.where(lax.broadcasted_iota(jnp.int32, (TOK_WIN, CHUNK), 0) == rel, 1.0, 0.0)
-        left = jnp.concatenate([hot, hi, hi, hi, mid, mid, lo], axis=0).astype(bf16)
         tok_at = pl.ds(pl.multiple_of(k * (CHUNK // 8), CHUNK // 8), TOK_WIN)
-        right = jnp.concatenate([tok[tok_at, :], coord_w], axis=0)
-        h = single[pl.ds(at, CHUNK), :].astype(f32) + dot(left, right, ((0,), (0,)))
+        h = hid[pl.ds(at, CHUNK), :] + dot(hots[pl.ds(at, CHUNK), 0:TOK_WIN], tok[tok_at, :])
         hid[pl.ds(at, CHUNK), :] = h
         project(0, at, h)
         return 0
@@ -350,39 +382,128 @@
             noisy = cx[:, pl.ds(at, size)]
             out = inv * (4.0 * noisy + (2.0 * sig) * update)
             pred[:, pl.ds(pl.multiple_of(at - HALO, 128), size)] = out
-            part = (at - HALO) // (half * PAIR_BLK)
+            first_block = (at - HALO) // PAIR_BLK
             for d in range(3):
-                for i in range(half):
-                    wide[d * half + i : d * half + i + 1, :] = out[
+                for i in range(size // PAIR_BLK):
+                    wide[pl.ds(d * blocks + first_block + i, 1), :] = out[
                         d : d + 1, i * PAIR_BLK : (i + 1) * PAIR_BLK
                     ]
-            pay[part] = wide[0 : 4 * half, :].astype(bf16)
-
-    middle = HALO + rows // 2
-    start = HALO - 128
-    end = HALO + rows + 128
-    block(0, start, middle + 256 - start)
-    block(1, start, middle + 128 - start)
-    block(2, HALO, rows // 2)
-    pred_gathers[0].start()
-    block(0, middle + 256, end - middle - 256)
-    pred_gathers[0].forward()
-    block(1, middle + 128, end - middle - 128)
-    block(2, middle, rows // 2)
-    pred_gathers[1].start()
-    pred_gathers[1].forward()
+
+    for layer in range(LAYERS):
+        low = HALO if layer == LAYERS - 1 else HALO - 128
+        size = (rows if layer == LAYERS - 1 else rows + 256) // 2
+
+        @pl.loop(0, 2)
+        def _(k, layer=layer, low=low, size=size):
+            block(layer, pl.multiple_of(low + k * size, 128), size)
+
+    pay[...] = wide[0 : 3 * blocks, :].astype(bf16)
+    pred_gather.start()
+
+    diagonal = lax.broadcasted_iota(jnp.int32, (PAIR_BLK, PAIR_BLK), 0) == lax.broadcasted_iota(
+        jnp.int32, (PAIR_BLK, PAIR_BLK), 1
+    )
+    none = jnp.zeros((16, PAIR_BLK), f32)
+
+    def within(group):
+        begun = []
+        for b in group:
+            at = slice(b * PAIR_BLK, (b + 1) * PAIR_BLK)
+            ours = [pred[d : d + 1, at] for d in range(3)]
+            known = [true[d : d + 1, at] for d in range(3)]
+            own = jnp.concatenate(
+                [
+                    jnp.concatenate([own_features(*ours), none], axis=1),
+                    jnp.concatenate([none, own_features(*known)], axis=1),
+                ],
+                axis=0,
+            ).astype(bf16)
+            owns[b] = own
+            part = jnp.concatenate(
+                [partner_features(*(v.astype(bf16).astype(f32) for v in vs)) for vs in (ours, known)],
+                axis=0,
+            ).astype(bf16)
+            begun.append((part[0:16], dot(part, own, ((0,), (0,)))))
+        coefs = [jnp.where(diagonal, 0.0, pair_coef(squares)).astype(bf16) for _, squares in begun]
+        for b, (part, _), coef in zip(group, begun, coefs):
+            selves[b] = dot(part, coef)[8:16]
+
+    within(range(blocks // 2))
+    pred_gather.forward()
+    within(range(blocks // 2, blocks))
+    for copy in parts + near + toks:
+        copy.wait_send()
+    for i, edge in enumerate(edges):
+        @pl.when(mine == edge[0])
+        def _(i=i):
+            for step in range(sample_peers):
+                edge_copy(i, step).wait_send()
+
     true_gather.finish()
-    pred_gathers[0].finish()
-    pred_gathers[1].finish()
+    pred_gather.finish()
 
 
 def pairs_kernel(
-    sigma, counts, partners, gathered_pred, gathered_true, pred, true,
-    coord_grad, lddt_grad, wide_pred, wide_true, owns, totals, held, parts,
+    sigma, counts, partners, gathered_pred, gathered_true, owns, selves, pred, true,
+    coord_grad, lddt_grad, wide_pred, wide_true, totals, held, parts,
 ):
     blocks = counts.shape[0]
     wide_pred[...] = gathered_pred[...].astype(f32)
     wide_true[...] = gathered_true[...].astype(f32)
+    totals[0:blocks] = selves[...]
+    totals[blocks] = jnp.zeros((8, PAIR_BLK), f32)
+
+    def rows_of(wide, base):
+        return partner_features(*(wide[pl.ds(base + d * blocks, 1), :] for d in range(3)))
+
+    def begin(b, m):
+        known = jnp.minimum(b, blocks - 1)
+        p = partners[known, m]
+        owner, place = p // blocks, p % blocks
+        part_pred = rows_of(wide_pred, owner * (3 * blocks) + place)
+        part_true = rows_of(wide_true, owner * (4 * blocks) + place)
+        part = jnp.concatenate([part_pred, part_true], axis=0).astype(bf16)
+        squares = dot(part, owns[known], ((0,), (0,)))
+        count = counts[known]
+        row = jnp.where(m < count, b, blocks)
+        last = m + 1 >= count
+        return part, squares, row, (jnp.where(last, jnp.minimum(b + 1, blocks), b), jnp.where(last, 1, m + 1))
+
+    def start(slot, b, m):
+        rows = []
+        for i in range(UNROLL):
+            part, squares, row, (b, m) = begin(b, m)
+            parts[slot, i] = part[0:16]
+            held[slot, i] = squares
+            rows.append(row)
+        return rows, (b, m)
+
+    def end(slot, rows):
+        coefs = [pair_coef(held[slot, i]).astype(bf16) for i in range(UNROLL)]
+        found = [dot(parts[slot, i], coef)[8:16] for i, coef in enumerate(coefs)]
+        for row, sums in zip(rows, found):
+            totals[row] = totals[row] + sums
+
+    def visit(_, carry):
+        rows, place = carry
+        more, place = start(1, *place)
+        end(0, rows)
+        rows, place = start(0, *place)
+        end(1, more)
+        return rows, place
+
+    live = jnp.maximum(counts[0] - 1, 1)
+    for b in range(1, blocks):
+        live = live + jnp.maximum(counts[b] - 1, 1)
+    groups = (live + UNROLL - 1) // UNROLL
+    rows, _ = lax.fori_loop(0, groups // 2, visit, start(0, jnp.int32(0), jnp.int32(1)))
+
+    @pl.when(groups % 2 == 1)
+    def _():
+        end(0, rows)
+
+    square = sigma[0] * sigma[0]
+    mse_scale = jnp.full((1, PAIR_BLK), square + 4.0, f32) / jnp.full((1, PAIR_BLK), 6.0 * square, f32)
     peers = gathered_true.shape[0] // (4 * blocks)
     listed = jnp.zeros((blocks, PAIR_BLK), f32)
     for peer in range(peers):
@@ -390,115 +511,12 @@
     listed = jnp.sum(listed, axis=0, keepdims=True)
     total_pairs = listed * (PAIR_BLK * PAIR_BLK) - float(PAIR_BLK * blocks * peers)
     pair_scale = -0.0625 * (blocks * peers * PAIR_BLK * PAIR_BLK) / total_pairs
-    row8 = lax.broadcasted_iota(jnp.int32, (8, PAIR_BLK), 0)
-    row4 = row8 & 3
-    diff = lax.broadcasted_iota(jnp.int32, (PAIR_BLK, PAIR_BLK), 0) - lax.broadcasted_iota(
-        jnp.int32, (PAIR_BLK, PAIR_BLK), 1
-    )
-
-    half = blocks // 2
-
-    def partner_rows(wide, base, stride):
-        x, y, z = (wide[pl.ds(base + d * stride, 1), :] for d in range(3))
-        n1, n2, n3 = pieces(x * x + y * y + z * z)
-        xyz = jnp.where(row4 == 0, x, jnp.where(row4 == 1, y, z))
-        upper = jnp.where(row4 == 3, jnp.where(row8 == 3, n1, n2), xyz)
-        ones = jnp.where(row8 < 7, 1.0, 0.0)
-        lower = jnp.where(row8 < 3, xyz, jnp.where(row8 == 3, n3, ones))
-        return jnp.concatenate([upper, lower], axis=0)
-
-    def own_rows(x, y, z):
-        n = x * x + y * y + z * z + 1.0
-        n1, n2, n3 = pieces(0.25 * n)
-        xp, yp, zp = pieces(-0.5 * x), pieces(-0.5 * y), pieces(-0.5 * z)
-
-        def xyz(i):
-            return jnp.where(row4 == 0, xp[i], jnp.where(row4 == 1, yp[i], zp[i]))
-
-        upper = jnp.where(row4 == 3, 0.25, jnp.where(row8 < 4, xyz(0), xyz(1)))
-        norms = jnp.where(row8 == 4, n1, jnp.where(row8 == 5, n2, n3))
-        norms = jnp.where(row8 == 7, 0.0, norms)
-        lower = jnp.where(row8 < 3, xyz(2), jnp.where(row8 == 3, 0.25, norms))
-        return jnp.concatenate([upper, lower], axis=0)
-
-    none = jnp.zeros((16, PAIR_BLK), f32)
-    square = sigma[0] * sigma[0]
-    mse_scale = jnp.full((1, PAIR_BLK), square + 4.0, f32) / jnp.full((1, PAIR_BLK), 6.0 * square, f32)
-    totals[...] = jnp.zeros_like(totals)
-    owns[blocks] = jnp.zeros(owns.shape[1:], bf16) + 1.0
-    for b in range(blocks):
-        at = slice(b * PAIR_BLK, (b + 1) * PAIR_BLK)
-        own_pred = own_rows(*(pred[d : d + 1, at] for d in range(3)))
-        own_true = own_rows(*(true[d : d + 1, at] for d in range(3)))
-        owns[b] = jnp.concatenate(
-            [
-                jnp.concatenate([own_pred, none], axis=1),
-                jnp.concatenate([none, own_true], axis=1),
-            ],
-            axis=0,
-        ).astype(bf16)
-
-    def begin(b, m):
-        known = jnp.minimum(b, blocks - 1)
-        p = partners[known, m]
-        owner, place = p // blocks, p % blocks
-        at = place // half * (peers * 4 * half) + owner * (4 * half) + place % half
-        part_pred = partner_rows(wide_pred, at, half)
-        part_true = partner_rows(wide_true, owner * (4 * blocks) + place, blocks)
-        part = jnp.concatenate([part_pred, part_true], axis=0).astype(bf16)
-        squares = dot(part, owns[b], ((0,), (0,)))
-        last = m + 1 >= counts[known]
-        after = jnp.where(last, jnp.minimum(b + 1, blocks), b), jnp.where(last, 0, m + 1)
-        return part, squares, after
-
-    def middle(squares, m):
-        sp, st = squares[:, :PAIR_BLK], squares[:, PAIR_BLK:]
-        rp = lax.rsqrt(sp)
-        gap = sp * rp - st * lax.rsqrt(st)
-        e2 = gap * gap + 0.0025
-        re = lax.rsqrt(e2)
-        err = e2 * re
-        th = [jnp.tanh(0.5 * t - err) for t in (0.5, 1.0, 2.0, 4.0)]
-        slope = 4.0 - (th[0] * th[0] + th[1] * th[1] + th[2] * th[2] + th[3] * th[3])
-        coef = slope * gap * (re * rp)
-        shut = jnp.where(m == 0, 0, 2 * PAIR_BLK)
-        return jnp.where(diff == shut, 0.0, coef).astype(bf16)
-
-    def start(slot, b, m):
-        begun = []
-        for i in range(UNROLL):
-            part, squares, after = begin(b, m)
-            parts[slot, i] = part[0:16]
-            held[slot, i] = squares
-            begun.append((b, m))
-            b, m = after
-        return begun, (b, m)
-
-    def end(slot, begun):
-        coefs = [middle(held[slot, i], m) for i, (_, m) in enumerate(begun)]
-        found = [(b, dot(parts[slot, i], coef)[8:16]) for i, ((b, _), coef) in enumerate(zip(begun, coefs))]
-        for at, sums in found:
-            totals[at] = totals[at] + sums
-
-    def visit(_, carry):
-        begun, place = carry
-        more, place = start(1, *place)
-        end(0, begun)
-        begun, place = start(0, *place)
-        end(1, more)
-        return begun, place
-
-    live = counts[0]
-    for b in range(1, blocks):
-        live = live + counts[b]
-    lax.fori_loop(0, (live + 2 * UNROLL - 1) // (2 * UNROLL), visit, start(0, jnp.int32(0), jnp.int32(0)))
-
     for b in range(blocks):
         at = slice(b * PAIR_BLK, (b + 1) * PAIR_BLK)
         total = totals[b]
         for d in range(3):
             pc, tc = pred[d : d + 1, at], true[d : d + 1, at]
-            lg = pair_scale[:, 0:PAIR_BLK] * (pc * total[4:5] - total[d : d + 1])
+            lg = pair_scale * (pc * total[4:5] - total[d : d + 1])
             lddt_grad[d, :, at] = lg
             coord_grad[d, :, at] = mse_scale * (pc - tc) - lg * (1.0 / PAIR_BLK)
 
@@ -527,29 +545,32 @@
         name="atoms",
         out_shape=(
             jax.ShapeDtypeStruct((8, rows), f32),
+            jax.ShapeDtypeStruct((atom_peers * 3 * blocks, PAIR_BLK), bf16),
             jax.ShapeDtypeStruct((atom_peers * 4 * blocks, PAIR_BLK), bf16),
-            jax.ShapeDtypeStruct((atom_peers * 4 * blocks, PAIR_BLK), bf16),
+            jax.ShapeDtypeStruct((blocks, 32, 2 * PAIR_BLK), bf16),
+            jax.ShapeDtypeStruct((blocks, 8, PAIR_BLK), f32),
         ),
         in_specs=smem(2) + vmem(13),
-        out_specs=tuple(vmem(3)),
+        out_specs=tuple(vmem(5)),
         scratch_shapes=[
             pltpu.VMEM((ext, CHANNELS), f32),
             pltpu.VMEM((2, ext, 2 * CHANNELS), bf16),
             pltpu.VMEM((2, ext // QBLK, CHANNELS, CHANNELS), bf16),
             pltpu.VMEM((ext, CHANNELS), f32),
-            pltpu.VMEM((2, 2 * blocks, PAIR_BLK), bf16),
+            pltpu.VMEM((3 * blocks, PAIR_BLK), bf16),
             pltpu.VMEM((4 * blocks, PAIR_BLK), bf16),
             pltpu.VMEM((4 * blocks, PAIR_BLK), f32),
             pltpu.VMEM((tokens + 2 * TOK_HALO, CHANNELS), bf16),
+            pltpu.VMEM((2, HALO, CHANNELS), bf16),
+            pltpu.VMEM((8, ext), f32),
             pltpu.VMEM((ext, CHANNELS), bf16),
-            pltpu.VMEM((8, ext), f32),
             pltpu.VMEM((tokens, CHANNELS), f32),
             pltpu.VMEM((sample_peers, part, CHANNELS), f32),
             pltpu.VMEM((part, CHANNELS), bf16),
             dma((sample_peers,)), dma((sample_peers,)), dma((sample_peers,)), dma((sample_peers,)),
-            dma((sample_peers,)), dma((4,)), dma((4,)), dma((4,)), dma,
+            dma((sample_peers,)), dma((4,)), dma((4,)), dma((4,)),
         ]
-        + 3 * one_gather,
+        + 2 * one_gather,
         compiler_params=pltpu.CompilerParams(
             collective_id=0, has_side_effects=True, vmem_limit_bytes=VMEM_LIMIT
         ),
@@ -559,25 +580,23 @@
     )
 
 
-def run_pairs(sigma, counts, partners, gathered_pred, gathered_true, pred, true):
+def run_pairs(sigma, counts, partners, gathered_pred, gathered_true, owns, selves, pred, true):
     rows = pred.shape[1]
-    wides = [pltpu.VMEM(g.shape, f32) for g in (gathered_pred, gathered_true)]
     out = jax.ShapeDtypeStruct((3, 1, rows), f32)
     coord_grad, lddt_grad = pl.pallas_call(
         pairs_kernel,
         name="pairs",
         out_shape=(out, out),
-        in_specs=smem(3) + vmem(4),
+        in_specs=smem(3) + vmem(6),
         out_specs=tuple(vmem(2)),
-        scratch_shapes=wides
+        scratch_shapes=[pltpu.VMEM(g.shape, f32) for g in (gathered_pred, gathered_true)]
         + [
-            pltpu.VMEM((rows // PAIR_BLK + 1, 32, 2 * PAIR_BLK), bf16),
             pltpu.VMEM((rows // PAIR_BLK + 1, 8, PAIR_BLK), f32),
             pltpu.VMEM((2, UNROLL, PAIR_BLK, 2 * PAIR_BLK), f32),
             pltpu.VMEM((2, UNROLL, 16, PAIR_BLK), bf16),
         ],
         compiler_params=pltpu.CompilerParams(vmem_limit_bytes=VMEM_LIMIT),
-    )(sigma, counts, partners, gathered_pred, gathered_true, pred, true)
+    )(sigma, counts, partners, gathered_pred, gathered_true, owns, selves, pred, true)
     return jnp.swapaxes(coord_grad, 0, 1), jnp.swapaxes(lddt_grad, 0, 1)
 
 
@@ -585,12 +604,12 @@
     token_feats, proj_w, atom_single, atom_token, true_coords, noise, sigma, coord_in,
     w_qkv, w_o, w_gu, w_down, gains, w_out, pair_blocks, pair_count,
 ):
-    pred, gathered_pred, gathered_true = run_atoms(
+    pred, gathered_pred, gathered_true, owns, selves = run_atoms(
         sigma, pair_count, token_feats.T, proj_w, atom_single, atom_token[None], true_coords,
         jnp.swapaxes(noise, 0, 1), coord_in, w_qkv, w_o, w_gu, w_down, gains, w_out,
     )
     return run_pairs(
-        sigma, pair_count, pair_blocks, gathered_pred, gathered_true, pred, true_coords
+        sigma, pair_count, pair_blocks, gathered_pred, gathered_true, owns, selves, pred, true_coords
     )
 
 

time: 70.1 us -> 65.8 us (0.939)
  Pallas kernels: 68.7 us -> 64.2 us
    pallas_call x1, Pallas kernels: 15.5 us -> 12.1 us  [run_pairs(): pl.pallas_call(pairs_kernel, name='pairs', out_shape=(out, out), in_specs...]
    pallas_call x1, Pallas kernels: 53.1 us -> 52.2 us  [run_atoms(): pl.pallas_call(functools.partial(atoms_kernel, atom_peers, sample_peers),...]
where the time goes in v5:
time: 65.8 us; the launch traced here: 65.5 us
  Pallas kernels  64.2 us (98%)
  between operations  1.29 us (2%)
    pallas_call x1, Pallas kernels, run_atoms(): pl.pallas_call(functools.partial(atoms_kernel, atom_peers, sample_peers),...  52.2 us
    pallas_call x1, Pallas kernels, run_pairs(): pl.pallas_call(pairs_kernel, name='pairs', out_shape=(out, out), in_specs...  12.1 us

profile of v5, /device:TPU:6, one launch (start us, length us, event | category | flops | bytes accessed | tf_op | source)
XLA Modules:
  0.0 65.5 jit_solution(5185526013670816070)
XLA Ops:
  1.3 52.2 %atoms.1 = (f32[8,2048]{1,0:T(8,128)}, bf16[1536,128]{1,0:T(8,128)(2,1)}, bf16[2048,128]{1,0:T(8,128)(2,1)}, bf16[16,32,256]{2,1,0:T(8,128)(2,1)}, f32[16,8,128]{2,1,0:T(8,128)}) custom-call(f32[1]{0:T(128)S(6)} %copy.18.sigma, s32[16]{0:T(128)} %counts.3, bf16[96,256]{1,0:T(8,128)(2,1)} %bitcast.6, bf16[96,128]{1,0:T(8,128)(2,1)} %proj.1, ...), custom_call_target="tpu_custom_call" | custom-call | tf_op jit(solution)/shard_map/atoms/pallas_call | solution.py:543
  53.4 12.1 %pairs.1 = (f32[3,1,2048]{2,1,0:T(1,128)}, f32[3,1,2048]{2,1,0:T(1,128)}) custom-call(f32[1]{0:T(128)S(6)} %copy.18.sigma, s32[16]{0:T(128)} %counts.3, s32[16,13]{1,0:T(8,128)} %partners.1, bf16[1536,128]{1,0:T(8,128)(2,1)} %get-tuple-element.9.gathered_pred, bf16[2048,128]{1,0:T(8,128)(2,1)} %get-tuple-element.10.gathered_true, ...), custom_call_target="tpu_custom_call" | custom-call | tf_op jit(solution)/shard_map/pairs/pallas_call | solution.py:586

commit v6 on v5

--- a/solution.py
+++ b/solution.py
@@ -98,6 +98,29 @@
             self.along_x(dx), self.mine,
         )
 
+    def line_copy(self, dx):
+        size = self.pay.shape[0] * self.nz
+        at = pl.ds(pl.multiple_of(self.me // self.nz * size, size), size)
+        line = self.whole.at[at]
+        return remote(line, line, self.x_send.at[dx], self.x_recv.at[dx], self.along_x(dx), self.mine)
+
+    def start_lines(self):
+        self.whole[self.rows(self.me), :] = self.pay[...]
+        for dz in self.order[1:]:
+            self.z_copy(dz).start()
+
+    def forward_lines(self):
+        for dz in self.order[1:]:
+            self.z_copy(dz).wait_recv()
+        for dx in range(1, self.nx):
+            self.line_copy(dx).start()
+
+    def finish_lines(self):
+        for dz in self.order[1:]:
+            self.z_copy(dz).wait_send()
+        for dx in range(1, self.nx):
+            self.line_copy(dx).wait()
+
     def start(self):
         for dz in self.order[1:]:
             self.z_copy(dz).start()
@@ -301,6 +324,7 @@
             for step in range(sample_peers):
                 edge_copy(i, step).start()
 
+    true_gather.start_lines()
     for copy in near:
         copy.wait_recv()
     prepare(0, near_single[0])
@@ -309,7 +333,6 @@
         copy.wait_recv()
     for i in range(len(edges)):
         edge_copy(i, 0).wait_recv()
-    true_gather.start()
 
     def project(layer, at, h):
         normed = (rms_scale(h) * gains[layer, 0:1, :]).astype(bf16)
@@ -339,7 +362,7 @@
 
     lax.fori_loop(0, ext // CHUNK, first, 0, unroll=FIRST_UNROLL)
 
-    true_gather.forward()
+    true_gather.forward_lines()
 
     def attend(layer, at, size):
         buf = layer % 2
@@ -439,7 +462,7 @@
             for step in range(sample_peers):
                 edge_copy(i, step).wait_send()
 
-    true_gather.finish()
+    true_gather.finish_lines()
     pred_gather.finish()
 
 

time: 65.8 us -> 64.8 us (0.985)
  Pallas kernels: 64.2 us -> 62.9 us
    pallas_call x1, Pallas kernels: 52.2 us -> 49.5 us  [run_atoms(): pl.pallas_call(functools.partial(atoms_kernel, atom_peers, sample_peers),...]
    pallas_call x1, Pallas kernels: 12.1 us -> 13.4 us  [run_pairs(): pl.pallas_call(pairs_kernel, name='pairs', out_shape=(out, out), in_specs...]
where the time goes in v6:
time: 64.8 us; the launch traced here: 64.2 us
  Pallas kernels  62.9 us (97%)
  between operations  1.29 us (2%)
    pallas_call x1, Pallas kernels, run_atoms(): pl.pallas_call(functools.partial(atoms_kernel, atom_peers, sample_peers),...  49.5 us
    pallas_call x1, Pallas kernels, run_pairs(): pl.pallas_call(pairs_kernel, name='pairs', out_shape=(out, out), in_specs...  13.4 us

profile of v6, /device:TPU:6, one launch (start us, length us, event | category | flops | bytes accessed | tf_op | source)
XLA Modules:
  0.0 64.2 jit_solution(5394066482659325449)
XLA Ops:
  1.3 49.5 %atoms.1 = (f32[8,2048]{1,0:T(8,128)}, bf16[1536,128]{1,0:T(8,128)(2,1)}, bf16[2048,128]{1,0:T(8,128)(2,1)}, bf16[16,32,256]{2,1,0:T(8,128)(2,1)}, f32[16,8,128]{2,1,0:T(8,128)}) custom-call(f32[1]{0:T(128)S(6)} %copy.18.sigma, s32[16]{0:T(128)} %counts.3, bf16[96,256]{1,0:T(8,128)(2,1)} %bitcast.6, bf16[96,128]{1,0:T(8,128)(2,1)} %proj.1, ...), custom_call_target="tpu_custom_call" | custom-call | tf_op jit(solution)/shard_map/atoms/pallas_call | solution.py:566
  50.7 13.4 %pairs.1 = (f32[3,1,2048]{2,1,0:T(1,128)}, f32[3,1,2048]{2,1,0:T(1,128)}) custom-call(f32[1]{0:T(128)S(6)} %copy.18.sigma, s32[16]{0:T(128)} %counts.3, s32[16,13]{1,0:T(8,128)} %partners.1, bf16[1536,128]{1,0:T(8,128)(2,1)} %get-tuple-element.9.gathered_pred, bf16[2048,128]{1,0:T(8,128)(2,1)} %get-tuple-element.10.gathered_true, ...), custom_call_target="tpu_custom_call" | custom-call | tf_op jit(solution)/shard_map/pairs/pallas_call | solution.py:609

commit v7 on v6

--- a/solution.py
+++ b/solution.py
@@ -89,15 +89,6 @@
             self.along_z(dz), self.mine,
         )
 
-    def x_copy(self, dz, dx):
-        at = self.rows(self.along_z(-dz))
-        src = self.pay if dz == 0 else self.whole.at[at]
-        slot = dz * self.nx + dx
-        return remote(
-            src, self.whole.at[at], self.x_send.at[slot], self.x_recv.at[slot],
-            self.along_x(dx), self.mine,
-        )
-
     def line_copy(self, dx):
         size = self.pay.shape[0] * self.nz
         at = pl.ds(pl.multiple_of(self.me // self.nz * size, size), size)
@@ -121,25 +112,48 @@
         for dx in range(1, self.nx):
             self.line_copy(dx).wait()
 
+    groups = ((0, 1), (1, 2), (3, 2), (5, 3))
+
+    def places(self, first, count):
+        size = self.pay.shape[0]
+        at = pl.multiple_of((self.me // self.nz * self.nz + first) * size, size)
+        return self.whole.at[pl.ds(at, count * size)]
+
+    def near_copy(self, i):
+        return remote(
+            self.pay, self.places(i, 1), self.z_send.at[i], self.z_recv.at[i],
+            self.along_z(self.order[i]), self.mine,
+        )
+
+    def group_copy(self, j, dx):
+        part = self.places(*self.groups[j])
+        slot = j * self.nx + dx
+        return remote(
+            part, part, self.x_send.at[slot], self.x_recv.at[slot], self.along_x(dx), self.mine
+        )
+
     def start(self):
-        for dz in self.order[1:]:
-            self.z_copy(dz).start()
+        size = self.pay.shape[0]
+        at = pl.multiple_of(self.me // self.nz * self.nz * size, size)
+        self.whole[pl.ds(at, size), :] = self.pay[...]
+        for i in range(1, self.nz):
+            self.near_copy(i).start()
         for dx in range(1, self.nx):
-            self.x_copy(0, dx).start()
-        self.whole[self.rows(self.me), :] = self.pay[...]
+            self.group_copy(0, dx).start()
 
     def forward(self):
-        for dz in self.order[1:]:
-            self.z_copy(dz).wait_recv()
+        for j, (first, count) in enumerate(self.groups[1:], 1):
+            for i in range(first, first + count):
+                self.near_copy(i).wait_recv()
             for dx in range(1, self.nx):
-                self.x_copy(dz, dx).start()
+                self.group_copy(j, dx).start()
 
     def finish(self):
-        for dz in self.order[1:]:
-            self.z_copy(dz).wait_send()
-        for dz in self.order:
+        for i in range(1, self.nz):
+            self.near_copy(i).wait_send()
+        for j in range(len(self.groups)):
             for dx in range(1, self.nx):
-                self.x_copy(dz, dx).wait()
+                self.group_copy(j, dx).wait()
 
 
 def partner_features(x, y, z):
@@ -203,10 +217,11 @@
 
     for step in range(1, sample_peers):
         greet(me, lax.rem(mine + step, sample_peers))
-    for step in range(sample_peers):
-        greet(left, lax.rem(mine + step, sample_peers))
-        greet(right, lax.rem(mine + step, sample_peers))
-
+    greet(left, mine)
+    greet(right, mine)
+    for owner in (0, 1):
+        greet(right, owner)
+        greet(left, sample_peers - 1 - owner)
     for dz in range(1, nz):
         greet(along_z(dz), mine)
     for dx in range(1, nx):
@@ -241,7 +256,9 @@
         wide[3 * blocks + b : 3 * blocks + b + 1, :] = jnp.full((1, PAIR_BLK), counts[b], jnp.int32).astype(f32)
     true_pay[...] = wide[...].astype(bf16)
     bias[...] = jnp.where((pos >= 0) & (pos < total_atoms), 0.0, -1e30)
-    pl.semaphore_wait(barrier, 3 * sample_peers - 1 + nz + nx - 2)
+    expected = sample_peers + 1 + nz + nx - 2
+    on_edge = (mine < 2) | (mine >= sample_peers - 2)
+    pl.semaphore_wait(barrier, expected + jnp.where(on_edge, sample_peers, 0))
     true_gather = Gather(atom_peers, true_pay, gathered_true, sems[8:12])
     pred_gather = Gather(atom_peers, pay, gathered_pred, sems[12:16])
 
@@ -473,6 +490,7 @@
     blocks = counts.shape[0]
     wide_pred[...] = gathered_pred[...].astype(f32)
     wide_true[...] = gathered_true[...].astype(f32)
+    here = partners[0, 0] // blocks
     totals[0:blocks] = selves[...]
     totals[blocks] = jnp.zeros((8, PAIR_BLK), f32)
 
@@ -483,7 +501,10 @@
         known = jnp.minimum(b, blocks - 1)
         p = partners[known, m]
         owner, place = p // blocks, p % blocks
-        part_pred = rows_of(wide_pred, owner * (3 * blocks) + place)
+        away = (here - owner) & (DEPTH - 1)
+        slot = jnp.where(away <= DEPTH // 2, jnp.maximum(2 * away - 1, 0), 2 * (DEPTH - away))
+        line = owner // DEPTH * DEPTH + slot
+        part_pred = rows_of(wide_pred, line * (3 * blocks) + place)
         part_true = rows_of(wide_true, owner * (4 * blocks) + place)
         part = jnp.concatenate([part_pred, part_true], axis=0).astype(bf16)
         squares = dot(part, owns[known], ((0,), (0,)))

time: 64.8 us -> 65 us (level)
  no operation moved by 1% of the time
where the time goes in v7:
time: 65 us; the launch traced here: 64.4 us
  Pallas kernels  63.1 us (97%)
  between operations  1.29 us (2%)
    pallas_call x1, Pallas kernels, run_atoms(): pl.pallas_call(functools.partial(atoms_kernel, atom_peers, sample_peers),...  49.1 us
    pallas_call x1, Pallas kernels, run_pairs(): pl.pallas_call(pairs_kernel, name='pairs', out_shape=(out, out), in_specs...  14 us

profile of v7, /device:TPU:6, one launch (start us, length us, event | category | flops | bytes accessed | tf_op | source)
XLA Modules:
  0.0 64.4 jit_solution(13332875010466700555)
XLA Ops:
  1.3 49.1 %atoms.1 = (f32[8,2048]{1,0:T(8,128)}, bf16[1536,128]{1,0:T(8,128)(2,1)}, bf16[2048,128]{1,0:T(8,128)(2,1)}, bf16[16,32,256]{2,1,0:T(8,128)(2,1)}, f32[16,8,128]{2,1,0:T(8,128)}) custom-call(f32[1]{0:T(128)S(6)} %copy.18.sigma, s32[16]{0:T(128)} %counts.3, bf16[96,256]{1,0:T(8,128)(2,1)} %bitcast.6, bf16[96,128]{1,0:T(8,128)(2,1)} %proj.1, ...), custom_call_target="tpu_custom_call" | custom-call | tf_op jit(solution)/shard_map/atoms/pallas_call | solution.py:587
  50.4 14.0 %pairs.1 = (f32[3,1,2048]{2,1,0:T(1,128)}, f32[3,1,2048]{2,1,0:T(1,128)}) custom-call(f32[1]{0:T(128)S(6)} %copy.18.sigma, s32[16]{0:T(128)} %counts.3, s32[16,13]{1,0:T(8,128)} %partners.1, bf16[1536,128]{1,0:T(8,128)(2,1)} %get-tuple-element.9.gathered_pred, bf16[2048,128]{1,0:T(8,128)(2,1)} %get-tuple-element.10.gathered_true, ...), custom_call_target="tpu_custom_call" | custom-call | tf_op jit(solution)/shard_map/pairs/pallas_call | solution.py:630

commit v8 on v7

--- a/solution.py
+++ b/solution.py
@@ -17,7 +17,7 @@
 PAIR_BLK = 128
 CHANNELS = 128
 CHUNK = 256
-FIRST_UNROLL = 5
+FIRST_UNROLL = 10
 UNROLL = 8
 HALO = 256
 TOK_HALO = 48
@@ -431,11 +431,7 @@
 
     for layer in range(LAYERS):
         low = HALO if layer == LAYERS - 1 else HALO - 128
-        size = (rows if layer == LAYERS - 1 else rows + 256) // 2
-
-        @pl.loop(0, 2)
-        def _(k, layer=layer, low=low, size=size):
-            block(layer, pl.multiple_of(low + k * size, 128), size)
+        block(layer, low, rows if layer == LAYERS - 1 else rows + 256)
 
     pay[...] = wide[0 : 3 * blocks, :].astype(bf16)
     pred_gather.start()

time: 65 us -> 62.4 us (0.960)
  Pallas kernels: 63.1 us -> 60.4 us
    pallas_call x1, Pallas kernels: 14 us -> 12.5 us  [run_pairs(): pl.pallas_call(pairs_kernel, name='pairs', out_shape=(out, out), in_specs...]
    pallas_call x1, Pallas kernels: 49.1 us -> 47.8 us  [run_atoms(): pl.pallas_call(functools.partial(atoms_kernel, atom_peers, sample_peers),...]
where the time goes in v8:
time: 62.4 us; the launch traced here: 61.7 us
  Pallas kernels  60.4 us (97%)
  between operations  1.29 us (2%)
    pallas_call x1, Pallas kernels, run_atoms(): pl.pallas_call(functools.partial(atoms_kernel, atom_peers, sample_peers),...  47.8 us
    pallas_call x1, Pallas kernels, run_pairs(): pl.pallas_call(pairs_kernel, name='pairs', out_shape=(out, out), in_specs...  12.5 us

profile of v8, /device:TPU:6, one launch (start us, length us, event | category | flops | bytes accessed | tf_op | source)
XLA Modules:
  0.0 61.7 jit_solution(6313727247389589318)
XLA Ops:
  1.3 47.8 %atoms.1 = (f32[8,2048]{1,0:T(8,128)}, bf16[1536,128]{1,0:T(8,128)(2,1)}, bf16[2048,128]{1,0:T(8,128)(2,1)}, bf16[16,32,256]{2,1,0:T(8,128)(2,1)}, f32[16,8,128]{2,1,0:T(8,128)}) custom-call(f32[1]{0:T(128)S(6)} %copy.18.sigma, s32[16]{0:T(128)} %counts.3, bf16[96,256]{1,0:T(8,128)(2,1)} %bitcast.6, bf16[96,128]{1,0:T(8,128)(2,1)} %proj.1, ...), custom_call_target="tpu_custom_call" | custom-call | tf_op jit(solution)/shard_map/atoms/pallas_call | solution.py:583
  49.1 12.5 %pairs.1 = (f32[3,1,2048]{2,1,0:T(1,128)}, f32[3,1,2048]{2,1,0:T(1,128)}) custom-call(f32[1]{0:T(128)S(6)} %copy.18.sigma, s32[16]{0:T(128)} %counts.3, s32[16,13]{1,0:T(8,128)} %partners.1, bf16[1536,128]{1,0:T(8,128)(2,1)} %get-tuple-element.9.gathered_pred, bf16[2048,128]{1,0:T(8,128)(2,1)} %get-tuple-element.10.gathered_true, ...), custom_call_target="tpu_custom_call" | custom-call | tf_op jit(solution)/shard_map/pairs/pallas_call | solution.py:626

commit v9 on v8

--- a/solution.py
+++ b/solution.py
@@ -430,8 +430,8 @@
                     ]
 
     for layer in range(LAYERS):
-        low = HALO if layer == LAYERS - 1 else HALO - 128
-        block(layer, low, rows if layer == LAYERS - 1 else rows + 256)
+        beyond = (128, 64, 0)[layer]
+        block(layer, HALO - beyond, rows + 2 * beyond)
 
     pay[...] = wide[0 : 3 * blocks, :].astype(bf16)
     pred_gather.start()

time: 62.4 us -> 63 us (level)
  Pallas kernels: 60.4 us -> 61.5 us
    pallas_call x1, Pallas kernels: 12.5 us -> 14 us  [run_pairs(): pl.pallas_call(pairs_kernel, name='pairs', out_shape=(out, out), in_specs...]
where the time goes in v9:
time: 63 us; the launch traced here: 62.8 us
  Pallas kernels  61.5 us (98%)
  between operations  1.29 us (2%)
    pallas_call x1, Pallas kernels, run_atoms(): pl.pallas_call(functools.partial(atoms_kernel, atom_peers, sample_peers),...  47.5 us
    pallas_call x1, Pallas kernels, run_pairs(): pl.pallas_call(pairs_kernel, name='pairs', out_shape=(out, out), in_specs...  14 us

profile of v9, /device:TPU:6, one launch (start us, length us, event | category | flops | bytes accessed | tf_op | source)
XLA Modules:
  0.0 62.8 jit_solution(15418952410776648419)
XLA Ops:
  1.3 47.5 %atoms.1 = (f32[8,2048]{1,0:T(8,128)}, bf16[1536,128]{1,0:T(8,128)(2,1)}, bf16[2048,128]{1,0:T(8,128)(2,1)}, bf16[16,32,256]{2,1,0:T(8,128)(2,1)}, f32[16,8,128]{2,1,0:T(8,128)}) custom-call(f32[1]{0:T(128)S(6)} %copy.18.sigma, s32[16]{0:T(128)} %counts.3, bf16[96,256]{1,0:T(8,128)(2,1)} %bitcast.6, bf16[96,128]{1,0:T(8,128)(2,1)} %proj.1, ...), custom_call_target="tpu_custom_call" | custom-call | tf_op jit(solution)/shard_map/atoms/pallas_call | solution.py:583
  48.8 14.0 %pairs.1 = (f32[3,1,2048]{2,1,0:T(1,128)}, f32[3,1,2048]{2,1,0:T(1,128)}) custom-call(f32[1]{0:T(128)S(6)} %copy.18.sigma, s32[16]{0:T(128)} %counts.3, s32[16,13]{1,0:T(8,128)} %partners.1, bf16[1536,128]{1,0:T(8,128)(2,1)} %get-tuple-element.9.gathered_pred, bf16[2048,128]{1,0:T(8,128)(2,1)} %get-tuple-element.10.gathered_true, ...), custom_call_target="tpu_custom_call" | custom-call | tf_op jit(solution)/shard_map/pairs/pallas_call | solution.py:626
